TPU v7x, 256 devices: a whole 4x4x8 slice. The times are simulated.
256 devices in a mesh: vocab: 64 (over y, z, core), hid: 4 (over x).
Axes of the slice: x: 4, y: 4, z: 8, core: 2. Of those that a mesh axis runs over, the one named last changes fastest.
Arguments:
- hidden: bfloat16 [768, 4096], P('vocab', 'hid'), may hold values from -40 to 40
- head_weight: bfloat16 [151936, 4096], P('vocab', 'hid'), may hold values from -1 to 1
- teacher_ids: int32 [768, 64], replicated, may hold values from 0 to 151935, as said below
- teacher_probs: float32 [768, 64], replicated, may hold values from 0.001 to 0.03
- token_weight: float32 [768], replicated, may hold values from 16 to 256
Outputs:
- grad_hidden: bfloat16 [768, 4096], P('vocab', 'hid')
- grad_weight: bfloat16 [151936, 4096], P('vocab', 'hid')
Inputs may be any that keep to these rules, and one draw needn't show every extreme that they name: `teacher_ids`: the 64 ids of a token are distinct.
All inputs are finite; a program needn't handle non-finite values.
Results may differ from a plain program's by a relative error of at most 0.0049.
Values may be sent and summed in bfloat16 or wider, within the bound.
A program may use at most 128 MiB of HBM per device.

v0:
```python
import jax
import jax.numpy as jnp
from jax import lax
from jax.sharding import PartitionSpec as P


def row_stats(logits):
    local_top = jnp.max(logits, axis=1)
    row_top = lax.pmax(local_top, "vocab")
    shifted = jnp.exp(logits - row_top[:, None])
    row_sum = lax.psum(jnp.sum(shifted, axis=1), "vocab")
    return (shifted, row_sum)


def logit_grad(logits, tok_ids, tok_probs, tok_weights, anchor):
    shifted, row_sum = row_stats(logits)
    tok_count = logits.shape[0]
    span_cols = logits.shape[1]
    local_ids = tok_ids - anchor
    inside = (local_ids >= 0) & (local_ids < span_cols)
    local_ids = jnp.where(inside, local_ids, span_cols)
    row_index = jnp.arange(tok_count, dtype=jnp.int32)[:, None]
    target = (
        jnp.zeros((tok_count, span_cols), jnp.float32)
        .at[row_index, local_ids]
        .add(tok_probs, mode="drop")
    )
    teacher_mass = jnp.sum(tok_probs, axis=1)
    return (
        tok_weights[:, None] * (teacher_mass[:, None] * shifted / row_sum[:, None] - target)
    ).astype(jnp.bfloat16)


def local(hidden, head_weight, teacher_ids, teacher_probs, token_weight):
    gathered = lax.all_gather(hidden, "vocab", axis=0, tiled=True)
    partial_value = lax.dot_general(
        gathered, head_weight, (((1,), (1,)), ((), ())), preferred_element_type=jnp.float32
    )
    anchor = lax.axis_index("vocab") * head_weight.shape[0]
    logits = lax.psum(partial_value, "hid")
    scores = logit_grad(logits, teacher_ids, teacher_probs, token_weight, anchor)
    grad_hidden = lax.psum_scatter(
        jnp.dot(scores, head_weight, preferred_element_type=jnp.float32),
        "vocab",
        scatter_dimension=0,
        tiled=True,
    ).astype(jnp.bfloat16)
    grad_weight = lax.dot_general(
        scores, gathered, (((0,), (0,)), ((), ())), preferred_element_type=jnp.float32
    ).astype(jnp.bfloat16)
    return (grad_hidden, grad_weight)


def solution(mesh):
    return jax.shard_map(
        local,
        mesh=mesh,
        in_specs=(P("vocab", "hid"), P("vocab", "hid"), P(), P(), P()),
        out_specs=(P("vocab", "hid"), P("vocab", "hid")),
        check_vma=False,
    )
```

profile of v0, /device:TPU:1, one launch (start us, length us, event | category | flops | bytes accessed | tf_op | source)
XLA Modules:
  0.0 858.9 jit_solution(15032600121887104542)
XLA Ops:
  7.9 84.4 %all-gather.3.cloned.1.call-done = bf16[64,12,1024]{2,1,0:T(8,128)(2,1)} async-done(((bf16[1,12,1024]{2,1,0:T(8,128)(2,1)}), bf16[64,12,1024]{2,1,0:T(8,128)(2,1)}) %all-gather.3.cloned.1.call-update) | async-done | bytes 1572880 | tf_op jit(solution)/shard_map/all_gather | solution.py:35
  92.4 2.5 reshape.21
  94.9 8.9 %fusion.8 = f32[768,2374]{0,1:T(8,128)} fusion(bf16[768,1024]{1,0:T(8,128)(2,1)S(1)} %reshape.21, bf16[2374,1024]{1,0:T(8,128)(2,1)} %param.6), kind=kOutput, calls=%fused_computation.17 | convolution fusion | flops 3733979136 | bytes 13727744 | tf_op jit(solution)/shard_map/dot_general | solution.py:36
  105.7 259.6 %scatter_custom_fusion = f32[1823232]{0:T(1024)} fusion(s32[49152]{0:T(1024)S(1)} %reshape.14, f32[49152]{0:T(1024)S(1)} %reshape.16, f32[]{:T(128)} %constant.6.clone.1), kind=kCustom, calls=%fused_computation.7 | custom fusion | flops 49152 | bytes 7292932
  365.3 9.0 %reshape.12 = f32[2374,768]{1,0:T(8,128)} reshape(f32[1823232]{0:T(1024)} %scatter_custom_fusion) | data formatting | bytes 14585856
  374.3 3.5 reduce_max.9
  377.9 123.7 %pmax.7 = f32[768]{0:T(1024)S(1)} all-reduce(f32[768]{0:T(1024)S(1)} %reduce_max.9), channel_id=1, replica_groups=mesh['vocab'=64,'hid'=4] {'vocab'}, use_global_device_ids=true, to_apply=%region_3.0 | all-reduce | flops 768 | bytes 6144 | tf_op jit(solution)/shard_map/pmax | solution.py:9
  501.5 4.1 fusion.3
  505.6 126.6 %psum.15 = f32[768]{0:T(1024)S(1)} all-reduce(f32[768]{0:T(1024)S(1)} %fusion.3), channel_id=1, replica_groups=mesh['vocab'=64,'hid'=4] {'vocab'}, use_global_device_ids=true, to_apply=%region_5.6 | all-reduce | flops 768 | bytes 6144 | tf_op jit(solution)/shard_map/psum | solution.py:11
  632.2 6.2 fusion.2
  638.4 1.8 copy-done
  640.3 6.2 fusion.9
  646.5 145.5 %fusion = f32[16,1024]{1,0:T(8,128)S(1)} fusion(f32[768,1024]{1,0:T(8,128)S(1)} %fusion.9), kind=kCustom, calls=%all-reduce-scatter | all-reduce-scatter fusion | flops 1048577 | bytes 3212288
  799.8 12.7 %collective-permute-start.9 = (bf16[16,1024]{1,0:T(8,128)(2,1)S(1)}, bf16[16,1024]{1,0:T(8,128)(2,1)S(1)}, u32[]{:S(2)}, u32[]{:S(2)}) collective-permute-start(bf16[16,1024]{1,0:T(8,128)(2,1)S(1)} %convert.30), channel_id=1, source_target_pairs={{0,40},{4,44},{8,48},{12,52},{16,56},{20,60},{24,64},{28,68},{32,7... | collective-permute-start | bytes 98312
  812.5 2.2 collective-permute-start.8
  814.7 1.6 collective-permute-start.7
  816.3 7.0 collective-permute-start.6
  825.9 4.0 collective-permute-start.4
  829.9 2.4 collective-permute-start.3
  832.3 2.9 collective-permute-start.2
  835.3 2.4 collective-permute-start.1
  837.7 2.7 collective-permute-start
  840.3 8.7 %convolution_convert_fusion = bf16[2374,1024]{1,0:T(8,128)(2,1)} fusion(bf16[768,2374]{0,1:T(8,128)(2,1)} %copy-done, bf16[768,1024]{1,0:T(8,128)(2,1)} %copy-done.1), kind=kOutput, calls=%fused_computation.6 | convolution fusion | flops 3736410112 | bytes 10081280 | tf_op jit(solution)/shard_map/dot_general | solution.py:48
  849.1 2.3 concatenate.4
  (57 shorter events, 12.9 us)
Async XLA Ops:
  7.2 85.2 %all-gather.3.cloned.1.call-start = ((), (), s32[]{:S(2)}) async-start(), calls=%async_computation.1 | async-start | bytes 2129920 | tf_op jit(solution)/shard_map/all_gather | solution.py:35
  7.9 366.4 %all-reduce.4.cloned.1.call-start = ((), (), s32[]{:S(2)}) async-start(), calls=%async_computation | async-start | bytes 14598144 | tf_op jit(solution)/shard_map/psum | solution.py:40
  94.9 8.9 %copy-start.1 = (bf16[768,1024]{1,0:T(8,128)(2,1)}, bf16[768,1024]{1,0:T(8,128)(2,1)S(1)}, u32[]{:S(2)}) copy-start(bf16[768,1024]{1,0:T(8,128)(2,1)S(1)} %reshape.21) | copy-start | bytes 4718596
  103.8 1.1 copy-start.5
  103.8 1.6 copy-start.2
  377.9 254.3 %copy-start.4 = (f32[768]{0:T(1024)S(1)}, f32[768]{0:T(1024)}, u32[]{:S(2)}) copy-start(f32[768]{0:T(1024)} %param.9) | copy-start | bytes 9220
  638.4 1.8 copy-start
  640.3 184.4 %copy-start.7 = (u32[256]{0:T(256)S(1)}, u32[256]{0:T(256)}, u32[]{:S(2)}) copy-start(u32[256]{0:T(256)} %constant.31) | copy-start | bytes 3076
  791.9 6.5 collective-permute-start.15
  793.3 6.5 collective-permute-start.14
  794.6 17.9 %collective-permute-start.13 = (bf16[16,1024]{1,0:T(8,128)(2,1)S(1)}, bf16[16,1024]{1,0:T(8,128)(2,1)S(1)}, u32[]{:S(2)}, u32[]{:S(2)}) collective-permute-start(bf16[16,1024]{1,0:T(8,128)(2,1)S(1)} %convert.30), channel_id=1, source_target_pairs={{0,56},{4,60},{8,64},{12,68},{16,72},{20,76},{24,80},{28,84},{32,8... | collective-permute-start | bytes 98312
  795.9 18.8 %collective-permute-start.12 = (bf16[16,1024]{1,0:T(8,128)(2,1)S(1)}, bf16[16,1024]{1,0:T(8,128)(2,1)S(1)}, u32[]{:S(2)}, u32[]{:S(2)}) collective-permute-start(bf16[16,1024]{1,0:T(8,128)(2,1)S(1)} %convert.30), channel_id=1, source_target_pairs={{0,52},{4,56},{8,60},{12,64},{16,68},{20,72},{24,76},{28,80},{32,8... | collective-permute-start | bytes 98312
  797.2 19.2 %collective-permute-start.11 = (bf16[16,1024]{1,0:T(8,128)(2,1)S(1)}, bf16[16,1024]{1,0:T(8,128)(2,1)S(1)}, u32[]{:S(2)}, u32[]{:S(2)}) collective-permute-start(bf16[16,1024]{1,0:T(8,128)(2,1)S(1)} %convert.30), channel_id=1, source_target_pairs={{0,48},{4,52},{8,56},{12,60},{16,64},{20,68},{24,72},{28,76},{32,8... | collective-permute-start | bytes 98312
  798.5 24.9 %collective-permute-start.10 = (bf16[16,1024]{1,0:T(8,128)(2,1)S(1)}, bf16[16,1024]{1,0:T(8,128)(2,1)S(1)}, u32[]{:S(2)}, u32[]{:S(2)}) collective-permute-start(bf16[16,1024]{1,0:T(8,128)(2,1)S(1)} %convert.30), channel_id=1, source_target_pairs={{0,44},{4,48},{8,52},{12,56},{16,60},{20,64},{24,68},{28,72},{32,7... | collective-permute-start | bytes 98312
  799.8 26.1 %collective-permute-start.9 = (bf16[16,1024]{1,0:T(8,128)(2,1)S(1)}, bf16[16,1024]{1,0:T(8,128)(2,1)S(1)}, u32[]{:S(2)}, u32[]{:S(2)}) collective-permute-start(bf16[16,1024]{1,0:T(8,128)(2,1)S(1)} %convert.30), channel_id=1, source_target_pairs={{0,40},{4,44},{8,48},{12,52},{16,56},{20,60},{24,64},{28,68},{32,7... | collective-permute-start | bytes 98312
  812.5 17.5 %collective-permute-start.8 = (bf16[16,1024]{1,0:T(8,128)(2,1)S(1)}, bf16[16,1024]{1,0:T(8,128)(2,1)S(1)}, u32[]{:S(2)}, u32[]{:S(2)}) collective-permute-start(bf16[16,1024]{1,0:T(8,128)(2,1)S(1)} %convert.30), channel_id=1, source_target_pairs={{0,36},{4,40},{8,44},{12,48},{16,52},{20,56},{24,60},{28,64},{32,6... | collective-permute-start | bytes 98312
  814.7 17.6 %collective-permute-start.7 = (bf16[16,1024]{1,0:T(8,128)(2,1)S(1)}, bf16[16,1024]{1,0:T(8,128)(2,1)S(1)}, u32[]{:S(2)}, u32[]{:S(2)}) collective-permute-start(bf16[16,1024]{1,0:T(8,128)(2,1)S(1)} %convert.30), channel_id=1, source_target_pairs={{0,32},{4,36},{8,40},{12,44},{16,48},{20,52},{24,56},{28,60},{32,6... | collective-permute-start | bytes 98312
  816.3 18.9 %collective-permute-start.6 = (bf16[16,1024]{1,0:T(8,128)(2,1)S(1)}, bf16[16,1024]{1,0:T(8,128)(2,1)S(1)}, u32[]{:S(2)}, u32[]{:S(2)}) collective-permute-start(bf16[16,1024]{1,0:T(8,128)(2,1)S(1)} %convert.30), channel_id=1, source_target_pairs={{0,28},{4,32},{8,36},{12,40},{16,44},{20,48},{24,52},{28,56},{32,6... | collective-permute-start | bytes 98312
  823.4 14.3 %collective-permute-start.5 = (bf16[16,1024]{1,0:T(8,128)(2,1)S(1)}, bf16[16,1024]{1,0:T(8,128)(2,1)S(1)}, u32[]{:S(2)}, u32[]{:S(2)}) collective-permute-start(bf16[16,1024]{1,0:T(8,128)(2,1)S(1)} %convert.30), channel_id=1, source_target_pairs={{0,24},{4,28},{8,32},{12,36},{16,40},{20,44},{24,48},{28,52},{32,5... | collective-permute-start | bytes 98312
  825.9 23.2 %collective-permute-start.4 = (bf16[16,1024]{1,0:T(8,128)(2,1)S(1)}, bf16[16,1024]{1,0:T(8,128)(2,1)S(1)}, u32[]{:S(2)}, u32[]{:S(2)}) collective-permute-start(bf16[16,1024]{1,0:T(8,128)(2,1)S(1)} %convert.30), channel_id=1, source_target_pairs={{0,20},{4,24},{8,28},{12,32},{16,36},{20,40},{24,44},{28,48},{32,5... | collective-permute-start | bytes 98312
  829.9 19.1 %collective-permute-start.3 = (bf16[16,1024]{1,0:T(8,128)(2,1)S(1)}, bf16[16,1024]{1,0:T(8,128)(2,1)S(1)}, u32[]{:S(2)}, u32[]{:S(2)}) collective-permute-start(bf16[16,1024]{1,0:T(8,128)(2,1)S(1)} %convert.30), channel_id=1, source_target_pairs={{0,16},{4,20},{8,24},{12,28},{16,32},{20,36},{24,40},{28,44},{32,4... | collective-permute-start | bytes 98312
  832.3 16.7 %collective-permute-start.2 = (bf16[16,1024]{1,0:T(8,128)(2,1)S(1)}, bf16[16,1024]{1,0:T(8,128)(2,1)S(1)}, u32[]{:S(2)}, u32[]{:S(2)}) collective-permute-start(bf16[16,1024]{1,0:T(8,128)(2,1)S(1)} %convert.30), channel_id=1, source_target_pairs={{0,12},{4,16},{8,20},{12,24},{16,28},{20,32},{24,36},{28,40},{32,4... | collective-permute-start | bytes 98312
  835.3 13.8 %collective-permute-start.1 = (bf16[16,1024]{1,0:T(8,128)(2,1)S(1)}, bf16[16,1024]{1,0:T(8,128)(2,1)S(1)}, u32[]{:S(2)}, u32[]{:S(2)}) collective-permute-start(bf16[16,1024]{1,0:T(8,128)(2,1)S(1)} %convert.30), channel_id=1, source_target_pairs={{0,8},{4,12},{8,16},{12,20},{16,24},{20,28},{24,32},{28,36},{32,40... | collective-permute-start | bytes 98312
  837.7 11.4 %collective-permute-start = (bf16[16,1024]{1,0:T(8,128)(2,1)S(1)}, bf16[16,1024]{1,0:T(8,128)(2,1)S(1)}, u32[]{:S(2)}, u32[]{:S(2)}) collective-permute-start(bf16[16,1024]{1,0:T(8,128)(2,1)S(1)} %convert.30), channel_id=1, source_target_pairs={{0,4},{4,8},{8,12},{12,16},{16,20},{20,24},{24,28},{28,32},{32,36}... | collective-permute-start | bytes 98312
  (2 other events, 1.9 us)
Sparse Core Ops, SparseCore 0:
  10.8 81.5 all-gather.2
  104.0 145.6 all-reduce.3
where the time goes:
time: 860 us; the launch traced here: 859 us
  blocking collectives  396 us (46%)
  other arithmetic  274 us (32%)
  waiting for transfers between devices  85.2 us (10%)
  starting transfers between devices  47 us (5%)
  matrix products  23.8 us (3%)
  local copies, waits for them, and re-layouts  18.3 us (2%)
  between operations  15.1 us (2%)
    unnamed x5, other arithmetic  260 us
    unnamed x1, blocking collectives  145 us
    psum x1, blocking collectives, row_stats(): row_sum = lax.psum(jnp.sum(shifted, axis=1), 'vocab')  127 us
    pmax x1, blocking collectives, row_stats(): row_top = lax.pmax(local_top, 'vocab')  124 us
    all_gather x1, waiting for transfers between devices, local(): gathered = lax.all_gather(hidden, 'vocab', axis=0, tiled=True)  84.4 us
    unnamed x16, starting transfers between devices  46.9 us
    unnamed x25, local copies, waits for them, and re-layouts  17.7 us
  transfers between devices with their start and end apart: 18, of which 1 were waited for; matrix products, arithmetic and copies ran while one was open for 32% of the time, Pallas kernels for 0%

commit v1 on v0

v1 whole, which is shorter than its diff:
```python
import functools

import jax
import jax.numpy as jnp
from jax import lax
from jax.experimental import pallas as pl
from jax.experimental.pallas import tpu as pltpu
from jax.sharding import PartitionSpec as P

MESH = pl.DeviceIdType.MESH
F32, BF16 = jnp.float32, jnp.bfloat16
NX, NY, NZ, NC = 4, 4, 8, 2
TOK, TOPK = 768, 64
NG, GT = 3, 256
VL, QR, BR = 2374, 608, 304
VP = NX * QR
DW = 1024
HD = DW // 2


def remote(src, dst, sems, index, device):
    return pltpu.make_async_remote_copy(
        src_ref=src, dst_ref=dst, send_sem=sems.at[(0, *index)], recv_sem=sems.at[(1, *index)],
        device_id=device, device_id_type=MESH,
    )


def kernel(
    hid_ref, w_ref, tail_ref, ids_ref, probs_ref, tw_ref, gw_ref, gh_ref,
    wv, wq, hp, hc, ex, tgt, st, stt, gw, gp, cb, ysum, yb, zsum, zb, fin, finb, outf,
    sown, sx, scr, sz, sy, fac,
    wl_sem, hl_sem, go_sem, xs, ws, ays, azs, bzs, bys, acs, bcs, es, fs, sxs, scs, szs, sys_, r1s, r2s, r3s, r4s,
):
    v = lax.axis_index("vocab")
    x = lax.axis_index("hid")
    y, z, c = v // (NZ * NC), lax.rem(v // NC, NZ), lax.rem(v, NC)

    def to(dx=0, dy=0, dz=0, dc=0):
        nx, ny = lax.rem(x + dx + NX, NX), lax.rem(y + dy + NY, NY)
        nz, nc = lax.rem(z + dz + NZ, NZ), lax.rem(c + dc, NC)
        return ((ny * NZ + nz) * NC + nc, nx)

    def px(d):
        return lax.rem(x + d + NX, NX)

    def py(d):
        return lax.rem(y + d + NY, NY)

    def pz(d):
        return lax.rem(z + d + NZ, NZ)

    pending = []

    def go(copy):
        copy.start()
        pending.append(copy)

    loads = []
    for k in range(NX):
        rows = QR if k < NX - 1 else 2368 - 3 * QR
        copy = pltpu.make_async_copy(w_ref.at[pl.ds(k * QR, rows)], wv.at[pl.ds(k * QR, rows)], wl_sem.at[k])
        copy.start()
        loads.append(copy)
    copy = pltpu.make_async_copy(tail_ref, wv.at[pl.ds(2368, 64)], wl_sem.at[NX])
    copy.start()
    loads.append(copy)

    def place_a(cc, zz, yy):
        return ((cc * NZ + zz) * NY + yy) * 2

    def place_b(cc, yy, zz):
        return 128 + ((cc * NY + yy) * NZ + zz) * 2

    def place(q):
        return jnp.where(q < 2, place_a(c, z, y), place_b(c, y, z)) + lax.rem(q, 2)

    own = pltpu.make_async_copy(hid_ref, hp.at[place(x)], hl_sem.at[0])
    own.start()

    peers = [dict(dx=d) for d in (1, 2, 3)] + [dict(dy=d) for d in (1, 2, 3)]
    peers += [dict(dz=d) for d in range(1, NZ)] + [dict(dc=1)]
    barrier = pltpu.get_barrier_semaphore()
    for peer in peers:
        pl.semaphore_signal(barrier, inc=1, device_id=to(**peer), device_id_type=MESH)
    pl.semaphore_wait(barrier, len(peers))

    for d in (1, 2, 3):
        go(remote(hid_ref, hp.at[place(x)], xs, (d - 1,), to(dx=d)))
    for copy in loads:
        copy.wait()

    def w_copy(b, d):
        q = px(d)
        return remote(
            wv.at[pl.ds(pl.multiple_of(q * QR + b * BR, 16), BR)], wq.at[d - 1, pl.ds(b * BR, BR)],
            ws, (b, d - 1), to(dx=d),
        )

    for b in range(2):
        for d in (1, 3, 2):
            go(w_copy(b, d))

    anchor = v * VL
    tw = tw_ref[...]

    def target(lo, hi):
        @pl.loop(lo * 6, hi * 6)
        def _(i):
            rows = pl.ds(pl.multiple_of((i // 6) * 128, 128), 128)
            lanes = pl.ds(pl.multiple_of(lax.rem(i, 6) * 128, 128), 128)
            index = lax.broadcasted_iota(jnp.int32, (128, 128), 0) + (anchor + (i // 6) * 128)
            total = jnp.zeros((128, 128), F32)
            for k in range(TOPK):
                total = jnp.where(ids_ref[pl.ds(k, 1), lanes] == index, probs_ref[pl.ds(k, 1), lanes], total)
            tgt[rows, lanes] = total * tw_ref[pl.ds(0, 1), lanes]

    target(0, 2)

    own.wait()
    for d in (1, 2, 3):
        at = hp.at[place(px(-d))]
        remote(at, at, xs, (d - 1,), to(dx=d)).wait_recv()

    def block(start, size):
        return hp.at[pl.ds(start, size)]

    def ay(dd, d):
        at = block(place_a(c, z, py(dd)), 2)
        return remote(at, at, ays, (d - 1,), to(dy=d))

    def az(origin, way, s):
        at = block(place_a(c, pz(origin), 0), 8)
        return remote(at, at, azs, (way, s - 1), to(dz=1 if way == 0 else -1))

    def bz(origin, way, s):
        at = block(place_b(c, y, pz(origin)), 2)
        return remote(at, at, bzs, (way, s - 1), to(dz=1 if way == 0 else -1))

    def by(dd, d):
        at = block(place_b(c, py(dd), 0), 16)
        return remote(at, at, bys, (d - 1,), to(dy=d))

    def ac(k, cc):
        at = block(place_a(cc, pz(k), 0), 8)
        return remote(at, at, acs, (k,), to(dc=1))

    def bc(k, cc):
        at = block(place_b(cc, py(k), 0), 16)
        return remote(at, at, bcs, (k,), to(dc=1))

    for d in (1, 3, 2):
        go(ay(0, d))
    go(bz(0, 0, 1))
    go(bz(0, 1, 1))
    target(2, 4)
    for s in range(1, 5):
        for way, sign in ((0, -1), (1, 1)):
            if s <= (4, 3)[way]:
                bz(sign * s, way, s).wait_recv()
                if s < (4, 3)[way]:
                    go(bz(sign * s, way, s + 1))
        if s == 2:
            for d in (1, 2, 3):
                ay(-d, d).wait_recv()
            go(az(0, 0, 1))
            go(az(0, 1, 1))
            go(ac(0, c))
        if s < 4:
            target(3 + s, 4 + s)
    for d in (1, 3, 2):
        go(by(0, d))
    go(bc(0, c))
    target(7, 9)
    for s in range(1, 5):
        for way, sign in ((0, -1), (1, 1)):
            if s <= (4, 3)[way]:
                az(sign * s, way, s).wait_recv()
                if s < (4, 3)[way]:
                    go(az(sign * s, way, s + 1))
                go(ac((sign * s) % NZ, c))
        if s < 4:
            target(8 + 2 * s - 1, 8 + 2 * s + 1)
    for d in (1, 3, 2):
        by(-d, d).wait_recv()
        go(bc((-d) % NY, c))
    target(15, 19)
    for k in range(NZ):
        ac(k, 1 - c).wait_recv()
    for k in range(NY):
        bc(k, 1 - c).wait_recv()

    row = lax.broadcasted_iota(jnp.int32, (3 * 64, 256), 0)
    col = lax.broadcasted_iota(jnp.int32, (3 * 64, 256), 1)
    g_, i_ = row // 64, lax.rem(row, 64)
    pick = lax.rem(i_ // 4, 2) * 128 + (i_ // 8) * 16 + 4 * g_ + lax.rem(i_, 4)
    perm = jnp.where(col == pick, 1.0, 0.0).astype(BF16)

    @pl.loop(0, NX * NY)
    def _(i):
        q, yy = i // NY, lax.rem(i, NY)
        parts = []
        for cc in range(NC):
            for zz in range(NZ):
                at = jnp.where(q < 2, place_a(cc, zz, yy), place_b(cc, yy, zz)) + lax.rem(q, 2)
                parts.append(hp[at])
        rows = jnp.dot(perm, jnp.concatenate(parts, axis=0), preferred_element_type=F32).astype(BF16)
        for g in range(NG):
            hc[q, pl.ds(pl.multiple_of(g * GT + yy * 64, 16), 64), :] = rows[g * 64:(g + 1) * 64]

    def logits(b):
        for d in (1, 2, 3):
            w_copy_recv = remote(
                wq.at[d - 1, pl.ds(b * BR, BR)], wq.at[d - 1, pl.ds(b * BR, BR)], ws, (b, d - 1), to(dx=d)
            )
            w_copy_recv.wait_recv()
        first = x * QR + b * BR

        @pl.loop(0, NG)
        def _(g):
            toks = pl.ds(pl.multiple_of(g * GT, GT), GT)
            nt = (((1,), (1,)), ((), ()))
            total = lax.dot_general(
                wv[pl.ds(pl.multiple_of(first, 16), BR), :], hc[x, toks, :], nt, preferred_element_type=F32
            )
            for d in (1, 2, 3):
                total += lax.dot_general(
                    wq[d - 1, pl.ds(b * BR, BR), :], hc[px(-d), toks, :], nt, preferred_element_type=F32
                )
            real = lax.broadcasted_iota(jnp.int32, (BR, GT), 0) + first < VL
            total = jnp.where(real, total, -1e30)
            top = jnp.max(total, axis=0, keepdims=True)
            shifted = jnp.exp(total - top)
            sown[pl.ds(b, 1), toks] = top
            sown[pl.ds(2 + b, 1), toks] = jnp.sum(shifted, axis=0, keepdims=True)
            ex[x, b, g] = shifted.astype(BF16)

    def e_copy(q, b, g, way):
        at = ex.at[q, b, g]
        return remote(at, at, es, (way, b, g), to(dx=1 if way == 0 else -1))

    def f_copy(q, b, g):
        at = ex.at[q, b, g]
        return remote(at, at, fs, (b, g), to(dx=1 if b == 0 else -1))

    def e_send(b, g):
        go(e_copy(x, b, g, 0))
        go(e_copy(x, b, g, 1))

    def e_forward(g):
        for b in range(2):
            e_copy(px(-1), b, g, 0).wait_recv()
            if b == 0:
                go(f_copy(px(-1), 0, g))
        for b in (1, 0):
            e_copy(px(1), b, g, 1).wait_recv()
            if b == 1:
                go(f_copy(px(1), 1, g))

    sown[...] = jnp.zeros_like(sown)
    logits(0)
    e_send(0, 0)
    e_send(0, 1)
    logits(1)

    def sx_copy(q, d):
        return remote(sown, sx.at[q], sxs, (d - 1,), to(dx=d))

    for d in (1, 3, 2):
        go(sx_copy(x, d))
    e_send(1, 0)
    e_send(1, 1)
    sx[x] = sown[...]
    for d in (1, 3, 2):
        sx_copy(px(-d), d).wait_recv()
    tops = [sx[q, pl.ds(b, 1), :] for q in range(NX) for b in range(2)]
    sums = [sx[q, pl.ds(2 + b, 1), :] for q in range(NX) for b in range(2)]

    def merge(tops, sums):
        top = functools.reduce(jnp.maximum, tops)
        return top, functools.reduce(jnp.add, [s * jnp.exp(t - top) for s, t in zip(sums, tops)])

    def spread(buf, sems, me, top, total, moves, slot):
        buf[me] = jnp.zeros((8, TOK), F32)
        buf[me, pl.ds(0, 1), :] = top
        buf[me, pl.ds(1, 1), :] = total
        for i, move in enumerate(moves):
            go(remote(buf.at[me], buf.at[me], sems, (i,), to(**move)))
        for i, move in enumerate(moves):
            at = buf.at[slot(move)]
            remote(at, at, sems, (i,), to(**move)).wait_recv()
        n = len(moves) + 1
        return merge([buf[k, pl.ds(0, 1), :] for k in range(n)], [buf[k, pl.ds(1, 1), :] for k in range(n)])

    top, total = merge(tops, sums)
    top, total = spread(scr, scs, c, top, total, [dict(dc=1)], lambda m: 1 - c)
    top, total = spread(sz, szs, z, top, total, [dict(dz=d) for d in range(1, NZ)], lambda m: pz(-m["dz"]))
    e_forward(0)
    e_send(0, 2)
    e_send(1, 2)
    top, total = spread(sy, sys_, y, top, total, [dict(dy=d) for d in range(1, NY)], lambda m: py(-m["dy"]))
    scale = tw * jnp.sum(probs_ref[...], axis=0, keepdims=True) / total
    for i in range(2 * NX):
        fac[pl.ds(i, 1), :] = scale * jnp.exp(tops[i] - top)
    e_forward(1)

    def scores(g):
        f_copy(px(2), 0, g).wait_recv()
        f_copy(px(2), 1, g).wait_recv()
        toks = pl.ds(g * GT, GT)

        @pl.loop(0, 2 * NX)
        def _(i):
            rows = pl.ds(pl.multiple_of(i * BR, 16), BR)
            e = ex[i // 2, lax.rem(i, 2), g].astype(F32)
            st[rows, :] = (fac[pl.ds(i, 1), toks] * e - tgt[rows, toks]).astype(BF16)

        @pl.loop(0, VP // 128)
        def _(i):
            at = pl.ds(pl.multiple_of(i * 128, 128), 128)
            stt[:, at] = st[at, :].T

        @pl.loop(0, DW // 256)
        def _(i):
            at = pl.ds(pl.multiple_of(i * 256, 256), 256)
            gp[g, :, at] = jnp.dot(stt[...], wv[:, at], preferred_element_type=F32)

    def half(cc):
        return pl.ds(pl.multiple_of(cc * HD, HD), HD)

    def r1(g, cc):
        return remote(gp.at[g, :, half(cc)], cb.at[g], r1s, (g,), to(dc=1))

    def r2(g, d):
        return remote(ysum.at[g, pl.ds(pl.multiple_of(py(d) * 64, 64), 64)], yb.at[g, d - 1], r2s, (g, d - 1), to(dy=d))

    def r3(g, d):
        return remote(zsum.at[g, pl.ds(pl.multiple_of(pz(d) * 8, 8), 8)], zb.at[g, d - 1], r3s, (g, d - 1), to(dz=d))

    def r4(g):
        return remote(fin.at[g], finb.at[g], r4s, (g,), to(dc=1))

    def start1(g):
        go(r1(g, 1 - c))

    def start2(g):
        r1(g, 1 - c).wait_recv()
        ysum[g] = gp[g, :, half(c)] + cb[g]
        for d in (1, 3, 2):
            go(r2(g, d))

    def start3(g):
        for d in (1, 3, 2):
            r2(g, d).wait_recv()
        zsum[g] = ysum[g, pl.ds(pl.multiple_of(y * 64, 64), 64), :] + yb[g, 0] + yb[g, 1] + yb[g, 2]
        for d in (1, 7, 2, 6, 3, 5, 4):
            go(r3(g, d))

    def start4(g):
        for d in range(1, NZ):
            r3(g, d).wait_recv()
        part = zsum[g, pl.ds(pl.multiple_of(z * 8, 8), 8), :]
        for d in range(1, NZ):
            part += zb[g, d - 1]
        fin[g] = part
        go(r4(g))

    def finish(g):
        r4(g).wait_recv()
        mine, other = fin[g], finb[g]
        left, right = jnp.where(c == 0, mine, other), jnp.where(c == 0, other, mine)
        for h, part in enumerate((left, right)):
            outf[pl.ds(4 * g, 4), pl.ds(h * HD, HD)] = jnp.where(c == 0, part[0:4], part[4:8])

    def gw_part(g, m):
        rows = pl.ds(m * QR, QR)
        part = jnp.dot(st[rows, :], hc[x, pl.ds(g * GT, GT), :], preferred_element_type=F32)
        if g == 0:
            gw[rows, :] = part
        elif g == 1:
            gw[rows, :] += part
        else:
            tiles = pl.ds(m * (QR // 16), QR // 16)
            hp[tiles] = (gw[rows, :] + part).astype(BF16).reshape(QR // 16, 16, DW)
            copy = pltpu.make_async_copy(hp.at[tiles], gw_ref.at[tiles], go_sem.at[m])
            copy.start()
            return copy

    scores(0)
    start1(0)
    for m in range(NX):
        gw_part(0, m)
    start2(0)
    e_forward(2)
    scores(1)
    start1(1)
    start3(0)
    for m in range(NX):
        gw_part(1, m)
    start2(1)
    start4(0)
    scores(2)
    start1(2)
    start3(1)
    for copy in pending:
        copy.wait_send()
    done = len(pending)
    outs = [gw_part(2, 0)]
    start2(2)
    outs.append(gw_part(2, 1))
    start4(1)
    start3(2)
    outs.append(gw_part(2, 2))
    finish(0)
    finish(1)
    outs.append(gw_part(2, 3))
    start4(2)
    finish(2)
    gh_ref[...] = outf[0:12, :].astype(BF16)
    for copy in outs:
        copy.wait()
    for copy in pending[done:]:
        copy.wait_send()


def local(hidden, head_weight, teacher_ids, teacher_probs, token_weight):
    def order(a):
        k = a.shape[1]
        return a.reshape(NY * NZ * NC, NG, 4, k).transpose(3, 1, 0, 2).reshape(k, TOK)

    hid = jnp.pad(hidden, ((0, 4), (0, 0)))
    tail = jnp.pad(head_weight[2368:], ((0, 58), (0, 0)))
    vmem, hbm = pl.BlockSpec(memory_space=pltpu.VMEM), pl.BlockSpec(memory_space=pl.ANY)
    dma = pltpu.SemaphoreType.DMA
    gw, gh = pl.pallas_call(
        kernel,
        out_shape=(
            jax.ShapeDtypeStruct((VP // 16, 16, DW), BF16),
            jax.ShapeDtypeStruct((12, DW), BF16),
        ),
        in_specs=[vmem, hbm, vmem, vmem, vmem, vmem],
        out_specs=(hbm, vmem),
        scratch_shapes=[
            pltpu.VMEM((VP, DW), BF16),
            pltpu.VMEM((3, QR, DW), BF16),
            pltpu.VMEM((256, 16, DW), BF16),
            pltpu.VMEM((NX, TOK, DW), BF16),
            pltpu.VMEM((NX, 2, NG, BR, GT), BF16),
            pltpu.VMEM((VP, TOK), F32),
            pltpu.VMEM((VP, GT), BF16),
            pltpu.VMEM((GT, VP), BF16),
            pltpu.VMEM((VP, DW), F32),
            pltpu.VMEM((NG, GT, DW), F32),
            pltpu.VMEM((NG, GT, HD), F32),
            pltpu.VMEM((NG, GT, HD), F32),
            pltpu.VMEM((NG, 3, 64, HD), F32),
            pltpu.VMEM((NG, 64, HD), F32),
            pltpu.VMEM((NG, 7, 8, HD), F32),
            pltpu.VMEM((NG, 8, HD), F32),
            pltpu.VMEM((NG, 8, HD), F32),
            pltpu.VMEM((16, DW), F32),
            pltpu.VMEM((8, TOK), F32),
            pltpu.VMEM((NX, 8, TOK), F32),
            pltpu.VMEM((NC, 8, TOK), F32),
            pltpu.VMEM((NZ, 8, TOK), F32),
            pltpu.VMEM((NY, 8, TOK), F32),
            pltpu.VMEM((8, TOK), F32),
            dma((5,)), dma((1,)), dma((4,)),
            dma((2, 3)), dma((2, 2, 3)), dma((2, 3)), dma((2, 2, 4)), dma((2, 2, 4)), dma((2, 3)), dma((2, 8)),
            dma((2, 4)), dma((2, 2, 2, 3)), dma((2, 2, 3)), dma((2, 3)), dma((2, 1)), dma((2, 7)), dma((2, 3)),
            dma((2, 3)), dma((2, 3, 3)), dma((2, 3, 7)), dma((2, 3)),
        ],
        compiler_params=pltpu.CompilerParams(
            collective_id=0, has_side_effects=True, vmem_limit_bytes=63 * 2**20
        ),
        name="head_backward",
    )(hid, head_weight, tail, order(teacher_ids), order(teacher_probs), order(token_weight[:, None]))
    return gh, gw.reshape(VP, DW)[:VL]


def solution(mesh):
    return jax.shard_map(
        local,
        mesh=mesh,
        in_specs=(P("vocab", "hid"), P("vocab", "hid"), P(), P(), P()),
        out_specs=(P("vocab", "hid"), P("vocab", "hid")),
        check_vma=False,
    )
```

time: 860 us -> 157 us (0.18)
  blocking collectives: 396 us -> 0 us
  other arithmetic: 274 us -> 0 us
  Pallas kernels: 0 us -> 142 us
  waiting for transfers between devices: 85.2 us -> 0 us
  starting transfers between devices: 47 us -> 0 us
  matrix products: 23.8 us -> 0 us
  between operations: 15.1 us -> 0.68 us
    unnamed x5 -> x0, other arithmetic: 260 us -> none
    unnamed x1 -> x0, blocking collectives: 145 us -> none
    pallas_call x0 -> x1, Pallas kernels: none -> 142 us  [local(): pl.pallas_call(kernel, out_shape=(jax.ShapeDtypeStruct((VP // 16, 16, DW)...]
    psum x1 -> x0, blocking collectives: 127 us -> none  [row_stats(): row_sum = lax.psum(jnp.sum(shifted, axis=1), 'vocab')]
    pmax x1 -> x0, blocking collectives: 124 us -> none  [row_stats(): row_top = lax.pmax(local_top, 'vocab')]
    all_gather x1 -> x0, waiting for transfers between devices: 84.4 us -> none  [local(): gathered = lax.all_gather(hidden, 'vocab', axis=0, tiled=True)]
    unnamed x16 -> x0, starting transfers between devices: 46.9 us -> none
    dot_general x3 -> x0, matrix products: 23.8 us -> none  [the longest x1 8.93 us: local(): lax.dot_general(gathered, head_weight, (((1,), (1,)), ((), ())), preferre...]
  transfers between devices with their start and end apart: 18 -> 0, of which waited for: 1 -> 0; matrix products, arithmetic and copies ran while one was open for 32% -> 0% of each run, Pallas kernels for 0% -> 0%
where the time goes in v1:
time: 157 us
  Pallas kernels  142 us (90%)
  local copies, waits for them, and re-layouts  14 us (9%)
    pallas_call x1, Pallas kernels, local(): pl.pallas_call(kernel, out_shape=(jax.ShapeDtypeStruct((VP // 16, 16, DW)...  142 us
    slice x1, local copies, waits for them, and re-layouts, local(): return (gh, gw.reshape(VP, DW)[:VL])  5.14 us

profile of v1, /device:TPU:1, one launch (start us, length us, event | category | flops | bytes accessed | tf_op | source)
XLA Modules:
  0.0 156.9 jit_solution(11900157383393636225)
XLA Ops:
  0.6 0.7 slice.6
  1.4 1.4 pad.8.hid_ref
  2.7 0.7 pad.9.tail_ref
  3.4 0.8 reshape_broadcast_in_dim.3
  4.2 0.7 reshape.26.tw_ref
  4.9 1.1 copy.9
  6.0 0.1 copy.10
  6.1 0.8 copy.14.ids_ref
  6.9 1.1 copy.11
  8.0 0.1 copy.12
  8.1 0.8 copy.15.probs_ref
  8.9 142.2 %head_backward.1 = (bf16[152,16,1024]{2,1,0:T(8,128)(2,1)}, bf16[12,1024]{1,0:T(8,128)(2,1)}) custom-call(bf16[16,1024]{1,0:T(8,128)(2,1)} %pad.8.hid_ref, bf16[2374,1024]{1,0:T(8,128)(2,1)} %w_ref.1, bf16[64,1024]{1,0:T(8,128)(2,1)} %pad.9.tail_ref, s32[64,768]{1,0:T(8,128)} %copy.14.ids_ref, f32[64,768]{1,0:T(8,128)} %copy.15.probs_ref, ...), custom_call_target="tpu_custom_call" | custom-call | tf_op jit(solution)/shard_map/head_backward/pallas_call | solution.py:434
  151.1 0.0 copy-start
  151.1 5.1 %slice.8 = bf16[2374,1024]{1,0:T(8,128)(2,1)} slice(bf16[2432,1024]{1,0:T(8,128)(2,1)} %bitcast.12), slice={[0:2374], [0:1024]} | slice | bytes 9723904 | tf_op jit(solution)/shard_map/slice | solution.py:477
  156.3 0.0 copy-done
  156.3 0.6 copy.17
  (1 shorter events, 0.0 us)
Async XLA Ops:
  151.1 5.2 %copy-start = (bf16[12,1024]{1,0:T(8,128)(2,1)S(1)}, bf16[12,1024]{1,0:T(8,128)(2,1)}, u32[]{:S(2)}) copy-start(bf16[12,1024]{1,0:T(8,128)(2,1)} %get-tuple-element.8) | copy-start | bytes 73732

commit v2 on v1

v2 whole, which is shorter than its diff:
```python
import functools

import jax
import jax.numpy as jnp
from jax import lax
from jax.experimental import pallas as pl
from jax.experimental.pallas import tpu as pltpu
from jax.sharding import PartitionSpec as P

MESH = pl.DeviceIdType.MESH
F32, BF16 = jnp.float32, jnp.bfloat16
NX, NY, NZ, NC = 4, 4, 8, 2
TOK, TOPK, UT = 768, 64, 128
GROUPS = ((0, 2, 4, 0), (2, 2, 4, 4), (4, 1, 2, 8), (5, 1, 2, 10))
NG = len(GROUPS)
VL, QR, BR = 2374, 608, 304
VP = NX * QR
DW = 1024
HD = DW // 2
PW = 768
NU = TOK // UT
NN, NT = (((1,), (0,)), ((), ())), (((1,), (1,)), ((), ()))


def dot(a, b, dims=NN):
    return lax.dot_general(a, b, dims, preferred_element_type=F32)


def remote(src, dst, sems, index, device):
    return pltpu.make_async_remote_copy(
        src_ref=src, dst_ref=dst, send_sem=sems.at[(0, *index)], recv_sem=sems.at[(1, *index)],
        device_id=device, device_id_type=MESH,
    )


def fold(a):
    return jnp.concatenate([a[:, u * UT:(u + 1) * UT] for u in range(NU)], axis=0)


def pieces(a):
    first = a.astype(BF16)
    rest = a - first.astype(F32)
    second = rest.astype(BF16)
    return first, second, (rest - second.astype(F32)).astype(BF16)


def kernel(
    hid_ref, edge_ref, w_ref, ids_ref, probs_ref, tw_ref, gw_ref, gh_ref,
    wv, wq, wt, pack, hp, hc, ex, tgt, st, gw, gp, cb, ysum, yb, zsum, zb, fin, finb, outf, ghs,
    sraw, sown, sx, scr, sz, sy, fac, idr, prr, twr, idp, wpp, vec,
    wl_sem, hl_sem, go_sem, xs, ws, ays, azs, bzs, bys, acs, bcs, es, fs, sxs, scs, szs, sys_, r1s, r2s, r3s, r4s,
):
    v = lax.axis_index("vocab")
    x = lax.axis_index("hid")
    y, z, c = v // (NZ * NC), lax.rem(v // NC, NZ), lax.rem(v, NC)

    def px(d):
        return lax.rem(x + d + NX, NX)

    def py(d):
        return lax.rem(y + d + NY, NY)

    def pz(d):
        return lax.rem(z + d + NZ, NZ)

    def to(dx=0, dy=0, dz=0, dc=0):
        return ((py(dy) * NZ + pz(dz)) * NC + lax.rem(c + dc, NC), px(dx))

    pending = []

    def go(copy):
        copy.start()
        pending.append(copy)

    loads = []
    for k in range(NX):
        rows = QR if k < NX - 1 else 2368 - 3 * QR
        loads.append(pltpu.make_async_copy(w_ref.at[pl.ds(k * QR, rows)], wv.at[pl.ds(k * QR, rows)], wl_sem.at[k]))
    smalls = [
        pltpu.make_async_copy(src, dst, hl_sem.at[i])
        for i, (src, dst) in enumerate(((ids_ref, idr), (probs_ref, prr), (tw_ref, twr)))
    ]
    for copy in loads + smalls:
        copy.start()

    def place_a(cc, zz, yy):
        return ((cc * NZ + zz) * NY + yy) * 2

    def place_b(cc, yy, zz):
        return 128 + ((cc * NY + yy) * NZ + zz) * 2

    def place(q):
        return jnp.where(q < 2, place_a(c, z, y), place_b(c, y, z)) + lax.rem(q, 2)

    pack[0:12, :] = hid_ref[:, 0:PW]
    for h in range(3):
        pack[12:16, 256 * h:256 * h + 256] = hid_ref[4 * h:4 * h + 4, PW:DW]
    hp[place(x)] = pack[...]
    edge = lax.broadcasted_iota(jnp.int32, (16, DW), 0) < VL - 2368
    wv[pl.ds(2368, 16), :] = jnp.where(edge, edge_ref[...], jnp.zeros((16, DW), BF16))
    wv[pl.ds(2384, 48), :] = jnp.zeros((48, DW), BF16)

    peers = [dict(dx=d) for d in (1, 2, 3)] + [dict(dy=d) for d in (1, 2, 3)]
    peers += [dict(dz=d) for d in range(1, NZ)] + [dict(dc=1)]
    barrier = pltpu.get_barrier_semaphore()
    for peer in peers:
        pl.semaphore_signal(barrier, inc=1, device_id=to(**peer), device_id_type=MESH)
    pl.semaphore_wait(barrier, len(peers))

    for d in (1, 2, 3):
        go(remote(pack, hp.at[place(x)], xs, (d - 1,), to(dx=d)))
    for copy in loads:
        copy.wait()

    def w_copy(b, d):
        q = px(d)
        return remote(
            wv.at[pl.ds(pl.multiple_of(q * QR + b * BR, 16), BR)], wq.at[d - 1, pl.ds(b * BR, BR)],
            ws, (b, d - 1), to(dx=d),
        )

    for b in range(2):
        for d in (1, 3, 2):
            go(w_copy(b, d))
    loaded = [pending.pop() for _ in range(6)]

    for copy in smalls:
        copy.wait()
    row = lax.broadcasted_iota(jnp.int32, (TOK, TOK), 0)
    col = lax.broadcasted_iota(jnp.int32, (TOK, TOK), 1)
    source = jnp.zeros((TOK, TOK), jnp.int32)
    for unit, units, per, first in GROUPS:
        i = col - unit * UT
        here = (i >= 0) & (i < units * UT)
        source = jnp.where(here, (i // per) * 12 + first + lax.rem(i, per), source)
    perm = jnp.where(row == source, 1.0, 0.0).astype(BF16)
    near = idr[...] - v * VL
    near = jnp.where((near >= 0) & (near < VL), near, 4095)
    low, high = (near & 255).astype(F32).astype(BF16), (near >> 8).astype(F32).astype(BF16)
    idp[...] = (dot(high, perm) * 256.0 + dot(low, perm)).astype(jnp.int32)
    probs = functools.reduce(jnp.add, [dot(a, perm) for a in pieces(prr[...])])
    tw = functools.reduce(jnp.add, [dot(a, perm) for a in pieces(twr[...].reshape(1, TOK))])
    wpp[...] = probs * tw
    vec[0:NU, :] = fold(tw * jnp.sum(probs, axis=0, keepdims=True))

    def target(lo, hi):
        @pl.loop(lo, hi)
        def _(i):
            rows = pl.ds(pl.multiple_of((i // 6) * BR, 16), BR)
            lanes = pl.ds(pl.multiple_of(lax.rem(i, 6) * 128, 128), 128)
            index = lax.broadcasted_iota(jnp.int16, (BR, 128), 0)
            total = jnp.zeros((BR, 128), BF16)
            for k in range(TOPK):
                here = (idp[pl.ds(k, 1), lanes] - (i // 6) * BR).astype(jnp.int16)
                mass = wpp[pl.ds(k, 1), lanes].astype(BF16)
                total = jnp.where(
                    jnp.broadcast_to(here, (BR, 128)) == index, jnp.broadcast_to(mass, (BR, 128)), total
                )
            tgt[rows, lanes] = total

    for d in (1, 2, 3):
        at = hp.at[place(px(-d))]
        remote(at, at, xs, (d - 1,), to(dx=d)).wait_recv()

    def block(start, size):
        return hp.at[pl.ds(start, size)]

    def ay(dd, d):
        at = block(place_a(c, z, py(dd)), 2)
        return remote(at, at, ays, (d - 1,), to(dy=d))

    def az(origin, way, s):
        at = block(place_a(c, pz(origin), 0), 8)
        return remote(at, at, azs, (way, s - 1), to(dz=1 if way == 0 else -1))

    def bz(origin, way, s):
        at = block(place_b(c, y, pz(origin)), 2)
        return remote(at, at, bzs, (way, s - 1), to(dz=1 if way == 0 else -1))

    def by(dd, d):
        at = block(place_b(c, py(dd), 0), 16)
        return remote(at, at, bys, (d - 1,), to(dy=d))

    def ac(k, cc):
        at = block(place_a(cc, pz(k), 0), 8)
        return remote(at, at, acs, (k,), to(dc=1))

    def bc(k, cc):
        at = block(place_b(cc, py(k), 0), 16)
        return remote(at, at, bcs, (k,), to(dc=1))

    def ring(make, s, cross=None):
        for way, sign, steps in ((0, -1, 4), (1, 1, 3)):
            if s <= steps:
                make(sign * s, way, s).wait_recv()
                if s < steps:
                    go(make(sign * s, way, s + 1))
                if cross is not None:
                    go(cross((sign * s) % NZ, c))

    for d in (1, 3, 2):
        go(ay(0, d))
    go(bz(0, 0, 1))
    go(bz(0, 1, 1))
    target(0, 5)
    ring(bz, 1)
    for d in (1, 2, 3):
        ay(-d, d).wait_recv()
    go(az(0, 0, 1))
    go(az(0, 1, 1))
    go(ac(0, c))
    target(5, 10)
    ring(bz, 2)
    target(10, 15)
    ring(bz, 3)
    ring(az, 1, ac)
    target(15, 20)
    ring(bz, 4)
    for d in (1, 3, 2):
        go(by(0, d))
    go(bc(0, c))
    target(20, 27)
    ring(az, 2, ac)
    target(27, 37)
    ring(az, 3, ac)
    target(37, 48)
    ring(az, 4, ac)
    for d in (1, 3, 2):
        by(-d, d).wait_recv()
        go(bc((-d) % NY, c))
    for k in range(NZ):
        ac(k, 1 - c).wait_recv()
    for k in range(NY):
        bc(k, 1 - c).wait_recv()

    kinds = [(per, first) for _, _, per, first in GROUPS]
    kinds += [(per, 12 + first % 4) for _, _, per, first in GROUPS]
    height = sum(16 * per for per, _ in kinds)
    row = lax.broadcasted_iota(jnp.int32, (height, 256), 0)
    col = lax.broadcasted_iota(jnp.int32, (height, 256), 1)
    pick = jnp.zeros((height, 256), jnp.int32)
    begins, start = [], 0
    for per, first in kinds:
        i = row - start
        here = (i >= 0) & (i < 16 * per)
        zz, rest = i // (2 * per), lax.rem(i, 2 * per)
        pick = jnp.where(here, (rest // per) * 128 + zz * 16 + first + lax.rem(rest, per), pick)
        begins.append(start)
        start += 16 * per
    perm = jnp.where(col == pick, 1.0, 0.0).astype(BF16)

    @pl.loop(0, NX * NY)
    def _(i):
        q, yy = i // NY, lax.rem(i, NY)
        parts = []
        for cc in range(NC):
            for zz in range(NZ):
                at = jnp.where(q < 2, place_a(cc, zz, yy), place_b(cc, yy, zz)) + lax.rem(q, 2)
                parts.append(hp[at])
        rows = dot(perm, jnp.concatenate(parts, axis=0)).astype(BF16)
        for g, (unit, _, per, first) in enumerate(GROUPS):
            n, h = 16 * per, 256 * (first // 4)
            here = pl.ds(pl.multiple_of(unit * UT + yy * n, 16), n)
            hc[q, here, 0:PW] = rows[begins[g]:begins[g] + n]
            hc[q, here, PW:DW] = rows[begins[NG + g]:begins[NG + g] + n, h:h + 256]

    def w_wait(b):
        for d in (1, 2, 3):
            at = wq.at[d - 1, pl.ds(b * BR, BR)]
            remote(at, at, ws, (b, d - 1), to(dx=d)).wait_recv()

    def logits(b):
        first = x * QR + b * BR

        @pl.loop(0, TOK // 256)
        def _(i):
            toks = pl.ds(pl.multiple_of(i * 256, 256), 256)
            total = dot(wv[pl.ds(pl.multiple_of(first, 16), BR), :], hc[x, toks, :], NT)
            for d in (1, 2, 3):
                total += dot(wq[d - 1, pl.ds(b * BR, BR), :], hc[px(-d), toks, :], NT)
            real = lax.broadcasted_iota(jnp.int32, (BR, 256), 0) + first < VL
            total = jnp.where(real, total, -1e30)
            top = jnp.max(total, axis=0, keepdims=True)
            shifted = jnp.exp(total - top)
            sraw[pl.ds(b, 1), toks] = top
            sraw[pl.ds(2 + b, 1), toks] = jnp.sum(shifted, axis=0, keepdims=True)
            shifted = shifted.astype(BF16)
            ex[x, b, 2 * i] = shifted[:, 0:128]
            ex[x, b, 2 * i + 1] = shifted[:, 128:256]

    def e_at(q, b, g):
        return ex.at[q, b, pl.ds(GROUPS[g][0], GROUPS[g][1])]

    def e_copy(q, b, g, way):
        at = e_at(q, b, g)
        return remote(at, at, es, (way, b, g), to(dx=1 if way == 0 else -1))

    def f_copy(q, b, g):
        at = e_at(q, b, g)
        return remote(at, at, fs, (b, g), to(dx=1 if b == 0 else -1))

    def e_send(b, g):
        go(e_copy(x, b, g, 0))
        go(e_copy(x, b, g, 1))

    def e_wait(b, g, way):
        e_copy(px(-1 if way == 0 else 1), b, g, way).wait_recv()

    def e_forward(b, g):
        e_wait(b, g, b)
        go(f_copy(px(-1 if b == 0 else 1), b, g))

    w_wait(0)
    logits(0)
    e_send(0, 0)
    @pl.loop(0, NX)
    def _(q):
        for i in range(0, QR, 128):
            n = min(128, QR - i)
            wt[q, :, i:i + n] = wv[pl.ds(pl.multiple_of(q * QR + i, 16), n), :].T

    w_wait(1)
    e_send(0, 1)
    logits(1)

    def sx_copy(q, d):
        return remote(sown, sx.at[q], sxs, (d - 1,), to(dx=d))

    for j in range(4):
        sown[j * NU:(j + 1) * NU, :] = fold(sraw[pl.ds(j, 1), :])
    for d in (1, 3, 2):
        go(sx_copy(x, d))
    e_send(1, 0)
    sx[x] = sown[...]
    e_forward(0, 0)
    e_send(1, 1)
    for d in (1, 3, 2):
        sx_copy(px(-d), d).wait_recv()
    tops = [sx[q, b * NU:(b + 1) * NU, :] for q in range(NX) for b in range(2)]
    sums = [sx[q, (2 + b) * NU:(3 + b) * NU, :] for q in range(NX) for b in range(2)]

    def merge(tops, sums):
        top = functools.reduce(jnp.maximum, tops)
        return top, functools.reduce(jnp.add, [s * jnp.exp(t - top) for s, t in zip(sums, tops)])

    def spread(buf, sems, me, top, total, moves, slot):
        buf[me] = jnp.zeros((16, UT), F32)
        buf[me, 0:NU, :] = top
        buf[me, NU:2 * NU, :] = total
        for i, move in enumerate(moves):
            go(remote(buf.at[me], buf.at[me], sems, (i,), to(**move)))
        for i, move in enumerate(moves):
            at = buf.at[slot(move)]
            remote(at, at, sems, (i,), to(**move)).wait_recv()
        n = len(moves) + 1
        return merge([buf[k, 0:NU, :] for k in range(n)], [buf[k, NU:2 * NU, :] for k in range(n)])

    top, total = merge(tops, sums)
    top, total = spread(scr, scs, c, top, total, [dict(dc=1)], lambda m: 1 - c)
    e_forward(1, 0)
    top, total = spread(sz, szs, z, top, total, [dict(dz=d) for d in range(1, NZ)], lambda m: pz(-m["dz"]))
    e_forward(0, 1)
    e_send(0, 2)
    e_send(1, 2)
    top, total = spread(sy, sys_, y, top, total, [dict(dy=d) for d in range(1, NY)], lambda m: py(-m["dy"]))
    scale = vec[0:NU, :] / total
    for i in range(2 * NX):
        fac[i, 0:NU, :] = scale * jnp.exp(tops[i] - top)

    def part(g, d):
        unit, units, _, _ = GROUPS[g]
        size = units * UT
        q = px(d)
        if d == 2:
            f_copy(q, 0, g).wait_recv()
            f_copy(q, 1, g).wait_recv()
        elif d != 0:
            e_wait(1 if d == -1 else 0, g, 0 if d == -1 else 1)
        base = q * QR
        for b in range(2):
            rows = pl.ds(pl.multiple_of(base + b * BR, 16), BR)
            for u in range(units):
                toks = pl.ds((unit + u) * UT, UT)
                e = ex[q, b, unit + u].astype(F32)
                score = fac[2 * q + b, pl.ds(unit + u, 1), :] * e - tgt[rows, toks].astype(F32)
                st[rows, u * UT:(u + 1) * UT] = score.astype(BF16)

        @pl.loop(0, 2)
        def _(i):
            at = pl.ds(pl.multiple_of(i * HD, HD), HD)
            term = dot(wt[q, at, :], st[pl.ds(pl.multiple_of(base, 16), QR), 0:size])
            if d == 0:
                gp[g][at, :] = term
            else:
                gp[g][at, :] += term

    def gw_part(g, d):
        unit, units, _, _ = GROUPS[g]
        size = units * UT
        rows = pl.ds(pl.multiple_of(px(d) * QR, 16), QR)
        term = dot(st[rows, 0:size], hc[x, pl.ds(unit * UT, size), :])
        if g == 0:
            gw[rows, :] = term
        elif g < NG - 1:
            gw[rows, :] += term
        else:
            wv[rows, :] = (gw[rows, :] + term).astype(BF16)
            copy = pltpu.make_async_copy(wv.at[rows], gw_ref.at[rows], go_sem.at[d % NX])
            copy.start()
            return copy

    def half(cc):
        return pl.ds(pl.multiple_of(cc * HD, HD), HD)

    def tall(g):
        return GROUPS[g][2] * 16

    def deep(g, zz):
        return pl.ds(pl.multiple_of((zz * GROUPS[g][2] * 2 // 8) * 8, 8), 8)

    def r1(g, cc):
        return remote(gp[g].at[half(cc)], cb[g], r1s, (g,), to(dc=1))

    def r2(g, d):
        n = tall(g)
        src = ysum[g].at[pl.ds(pl.multiple_of(py(d) * n, 8), n)]
        return remote(src, yb.at[g, d - 1, pl.ds(0, n)], r2s, (g, d - 1), to(dy=d))

    def r3(g, d):
        return remote(zsum.at[g, deep(g, pz(d))], zb.at[g, d - 1], r3s, (g, d - 1), to(dz=d))

    def r4(g):
        return remote(fin.at[g], finb.at[g], r4s, (g,), to(dc=1))

    def start1(g):
        go(r1(g, 1 - c))

    def start2(g):
        r1(g, 1 - c).wait_recv()
        ysum[g][...] = (gp[g][half(c), :] + cb[g][...]).T
        for d in (1, 3, 2):
            go(r2(g, d))

    def start3(g):
        n = tall(g)
        for d in (1, 3, 2):
            r2(g, d).wait_recv()
        mine = ysum[g][pl.ds(pl.multiple_of(y * n, 8), n), :]
        zsum[g, 0:n] = mine + yb[g, 0, 0:n] + yb[g, 1, 0:n] + yb[g, 2, 0:n]
        for d in (1, 7, 2, 6, 3, 5, 4):
            go(r3(g, d))

    def start4(g):
        for d in range(1, NZ):
            r3(g, d).wait_recv()
        term = zsum[g, deep(g, z), :]
        for d in range(1, NZ):
            term += zb[g, d - 1]
        fin[g] = term
        go(r4(g))

    def finish(g):
        _, _, per, first = GROUPS[g]
        r4(g).wait_recv()
        mine, other = fin[g], finb[g]
        left, right = jnp.where(c == 0, mine, other), jnp.where(c == 0, other, mine)
        for h, a in enumerate((left, right)):
            a = jnp.where(c == 0, a, jnp.concatenate([a[per:], a[:per]], axis=0))
            if per == 2:
                a = jnp.where(lax.rem(z, 2) == 0, a, jnp.concatenate([a[4:], a[:4]], axis=0))
            outf[first:first + per, h * HD:(h + 1) * HD] = a[:per]

    part(0, 0)
    e_forward(1, 1)
    part(0, -1)
    part(0, 1)
    part(0, 2)
    start1(0)
    e_send(0, 3)
    e_send(1, 3)
    for d in (0, -1, 1, 2):
        gw_part(0, d)
    part(1, 0)
    e_forward(0, 2)
    part(1, -1)
    part(1, 1)
    start2(0)
    e_forward(1, 2)
    part(1, 2)
    start1(1)
    for d in (0, -1, 1, 2):
        gw_part(1, d)
    e_forward(0, 3)
    e_forward(1, 3)
    part(2, 0)
    part(2, -1)
    part(2, 1)
    part(2, 2)
    start1(2)
    start2(1)
    for d in (0, -1, 1, 2):
        gw_part(2, d)
    part(3, 0)
    part(3, -1)
    part(3, 1)
    start3(0)
    start2(2)
    part(3, 2)
    start1(3)
    for copy in loaded:
        copy.wait_send()
    outs = [gw_part(3, 0)]
    start3(1)
    outs.append(gw_part(3, -1))
    start2(3)
    start4(0)
    outs.append(gw_part(3, 1))
    start3(2)
    start4(1)
    outs.append(gw_part(3, 2))
    finish(0)
    start3(3)
    start4(2)
    finish(1)
    start4(3)
    finish(2)
    finish(3)
    ghs[...] = outf[0:12, :].astype(BF16)
    outs.append(pltpu.make_async_copy(ghs, gh_ref, go_sem.at[NX]))
    outs[-1].start()
    for copy in outs:
        copy.wait()
    for copy in pending:
        copy.wait_send()


def results(gw_ref, gh_ref, gw_out, gh_out, sems):
    copies = [pltpu.make_async_copy(gh_ref, gh_out, sems.at[5])]
    for i, (start, rows) in enumerate(((0, QR), (QR, QR), (2 * QR, QR), (3 * QR, 2368 - 3 * QR), (2368, VL - 2368))):
        here = pl.ds(start, rows)
        copies.append(pltpu.make_async_copy(gw_ref.at[here], gw_out.at[here], sems.at[i]))
    for copy in copies:
        copy.start()
    for copy in copies:
        copy.wait()


def local(hidden, head_weight, teacher_ids, teacher_probs, token_weight):
    hbm = pl.BlockSpec(memory_space=pl.ANY)
    dma = pltpu.SemaphoreType.DMA
    gw, gh = pl.pallas_call(
        kernel,
        grid=(1,),
        out_shape=(pltpu.VMEM((VP, DW), BF16), pltpu.VMEM((12, DW), BF16)),
        in_specs=[
            pl.BlockSpec((12, DW), lambda i: (0, 0)),
            pl.BlockSpec((16, DW), lambda i: (2368 // 16, 0)),
            hbm, hbm, hbm, hbm,
        ],
        out_specs=(hbm, hbm),
        scratch_shapes=[
            pltpu.VMEM((VP, DW), BF16),
            pltpu.VMEM((3, QR, DW), BF16),
            pltpu.VMEM((NX, DW, QR), BF16),
            pltpu.VMEM((16, PW), BF16),
            pltpu.VMEM((256, 16, PW), BF16),
            pltpu.VMEM((NX, TOK, DW), BF16),
            pltpu.VMEM((NX, 2, TOK // UT, BR, UT), BF16),
            pltpu.VMEM((VP, TOK), BF16),
            pltpu.VMEM((VP, 256), BF16),
            pltpu.VMEM((VP, DW), F32),
            [pltpu.VMEM((DW, n * UT), F32) for _, n, _, _ in GROUPS],
            [pltpu.VMEM((HD, n * UT), F32) for _, n, _, _ in GROUPS],
            [pltpu.VMEM((n * UT, HD), F32) for _, n, _, _ in GROUPS],
            pltpu.VMEM((NG, 3, 64, HD), F32),
            pltpu.VMEM((NG, 64, HD), F32),
            pltpu.VMEM((NG, 7, 8, HD), F32),
            pltpu.VMEM((NG, 8, HD), F32),
            pltpu.VMEM((NG, 8, HD), F32),
            pltpu.VMEM((16, DW), F32),
            pltpu.VMEM((12, DW), BF16),
            pltpu.VMEM((8, TOK), F32),
            pltpu.VMEM((4 * NU, UT), F32),
            pltpu.VMEM((NX, 4 * NU, UT), F32),
            pltpu.VMEM((NC, 16, UT), F32),
            pltpu.VMEM((NZ, 16, UT), F32),
            pltpu.VMEM((NY, 16, UT), F32),
            pltpu.VMEM((2 * NX, 8, UT), F32),
            pltpu.VMEM((TOPK, TOK), jnp.int32),
            pltpu.VMEM((TOPK, TOK), F32),
            pltpu.VMEM((TOK,), F32),
            pltpu.VMEM((TOPK, TOK), jnp.int32),
            pltpu.VMEM((TOPK, TOK), F32),
            pltpu.VMEM((8, UT), F32),
            dma((4,)), dma((3,)), dma((5,)),
            dma((2, 3)), dma((2, 2, 3)), dma((2, 3)), dma((2, 2, 4)), dma((2, 2, 4)), dma((2, 3)), dma((2, 8)),
            dma((2, 4)), dma((2, 2, 2, NG)), dma((2, 2, NG)), dma((2, 3)), dma((2, 1)), dma((2, 7)), dma((2, 3)),
            dma((2, NG)), dma((2, NG, 3)), dma((2, NG, 7)), dma((2, NG)),
        ],
        compiler_params=pltpu.CompilerParams(
            collective_id=0, has_side_effects=True, vmem_limit_bytes=58 * 2**20
        ),
        name="head_backward",
    )(hidden, head_weight, head_weight, teacher_ids.T, teacher_probs.T, token_weight)
    gw, gh = pl.pallas_call(
        results,
        out_shape=(jax.ShapeDtypeStruct((VL, DW), BF16), jax.ShapeDtypeStruct((12, DW), BF16)),
        in_specs=[hbm, hbm],
        out_specs=(hbm, hbm),
        scratch_shapes=[dma((6,))],
        compiler_params=pltpu.CompilerParams(vmem_limit_bytes=2**20),
        name="results",
    )(gw, gh)
    return gh, gw


def solution(mesh):
    return jax.shard_map(
        local,
        mesh=mesh,
        in_specs=(P("vocab", "hid"), P("vocab", "hid"), P(), P(), P()),
        out_specs=(P("vocab", "hid"), P("vocab", "hid")),
        check_vma=False,
    )
```

time: 157 us -> 127 us (0.81)
  Pallas kernels: 142 us -> 126 us
  local copies, waits for them, and re-layouts: 14 us -> 0 us
    pallas_call x1 -> x2, Pallas kernels: 142 us -> 126 us  [the longest x1 124 us: local(): pl.pallas_call(kernel, grid=(1,), out_shape=(pltpu.VMEM((VP, DW), BF16),...]
    slice x2 -> x0, local copies, waits for them, and re-layouts: 5.87 us -> none  [the longest x1 5.14 us: local(): return (gh, gw.reshape(VP, DW)[:VL])]
    unnamed x5 -> x0, local copies, waits for them, and re-layouts: 2.8 us -> none
    reshape x3 -> x0, local copies, waits for them, and re-layouts: 2.37 us -> none  [order(): a.reshape(NY * NZ * NC, NG, 4, k).transpose(3, 1, 0, 2).reshape(k, TOK)]
    pad x2 -> x0, local copies, waits for them, and re-layouts: 2.06 us -> none  [the longest x1 1.38 us: local(): hid = jnp.pad(hidden, ((0, 4), (0, 0)))]
where the time goes in v2:
time: 127 us
  Pallas kernels  126 us (99%)
    pallas_call x1, Pallas kernels, local(): pl.pallas_call(kernel, grid=(1,), out_shape=(pltpu.VMEM((VP, DW), BF16),...  124 us

profile of v2, /device:TPU:1, one launch (start us, length us, event | category | flops | bytes accessed | tf_op | source)
XLA Modules:
  0.0 127.3 jit_solution(13260935734648230623)
XLA Ops:
  0.6 124.2 %head_backward.1 = (bf16[2432,1024]{1,0:T(8,128)(2,1)S(1)}, bf16[12,1024]{1,0:T(8,128)(2,1)S(1)}) custom-call(bf16[12,1024]{1,0:T(8,128)(2,1)} %hid_ref.1, bf16[2374,1024]{1,0:T(8,128)(2,1)} %w_ref.1, bf16[2374,1024]{1,0:T(8,128)(2,1)} %w_ref.1, s32[64,768]{1,0:T(8,128)} %bitcast.2, f32[64,768]{1,0:T(8,128)} %bitcast.3, f32[768]{0:T(1024)} %tw_ref.1), custom_call_target="tpu_custom_call" | custom-call | tf_op jit(solution)/shard_map/head_backward/pallas_call | solution.py:551
  124.8 2.3 %results.1 = (bf16[2374,1024]{1,0:T(8,128)(2,1)}, bf16[12,1024]{1,0:T(8,128)(2,1)}) custom-call(bf16[2432,1024]{1,0:T(8,128)(2,1)S(1)} %get-tuple-element.6.gw_ref, bf16[12,1024]{1,0:T(8,128)(2,1)S(1)} %get-tuple-element.7.gh_ref), custom_call_target="tpu_custom_call" | custom-call | tf_op jit(solution)/shard_map/results/pallas_call | solution.py:605

commit v3 on v2

--- a/solution.py
+++ b/solution.py
@@ -46,7 +46,7 @@
 
 def kernel(
     hid_ref, edge_ref, w_ref, ids_ref, probs_ref, tw_ref, gw_ref, gh_ref,
-    wv, wq, wt, pack, hp, hc, ex, tgt, st, gw, gp, cb, ysum, yb, zsum, zb, fin, finb, outf, ghs,
+    wv, wq, wta, wtb, pack, hp, hc, ex, tgt, st, gw, gp, cb, ysum, ysb, yb, zsum, zb, fin, finb, outf, ghs,
     sraw, sown, sx, scr, sz, sy, fac, idr, prr, twr, idp, wpp, vec,
     wl_sem, hl_sem, go_sem, xs, ws, ays, azs, bzs, bys, acs, bcs, es, fs, sxs, scs, szs, sys_, r1s, r2s, r3s, r4s,
 ):
@@ -56,6 +56,8 @@
 
     def px(d):
         return lax.rem(x + d + NX, NX)
+
+    slots = (0, -1, 1, 2)
 
     def py(d):
         return lax.rem(y + d + NY, NY)
@@ -312,15 +314,20 @@
 
     w_wait(0)
     logits(0)
+    for i in range(0, 3 * QR, 128):
+        pieces_, j = [], i
+        while j < min(i + 128, 3 * QR):
+            k = j // QR
+            n = min(i + 128, 3 * QR, (k + 1) * QR) - j
+            pieces_.append(wv[pl.ds(pl.multiple_of(px(slots[k]) * QR + j - k * QR, 16), n), :])
+            j += n
+        wta[:, i:j] = jnp.concatenate(pieces_, axis=0).T
+    for i in range(0, QR, 128):
+        n = min(128, QR - i)
+        wtb[:, i:i + n] = wv[pl.ds(pl.multiple_of(px(2) * QR + i, 16), n), :].T
+
+    w_wait(1)
     e_send(0, 0)
-    @pl.loop(0, NX)
-    def _(q):
-        for i in range(0, QR, 128):
-            n = min(128, QR - i)
-            wt[q, :, i:i + n] = wv[pl.ds(pl.multiple_of(q * QR + i, 16), n), :].T
-
-    w_wait(1)
-    e_send(0, 1)
     logits(1)
 
     def sx_copy(q, d):
@@ -332,8 +339,6 @@
         go(sx_copy(x, d))
     e_send(1, 0)
     sx[x] = sown[...]
-    e_forward(0, 0)
-    e_send(1, 1)
     for d in (1, 3, 2):
         sx_copy(px(-d), d).wait_recv()
     tops = [sx[q, b * NU:(b + 1) * NU, :] for q in range(NX) for b in range(2)]
@@ -343,69 +348,74 @@
         top = functools.reduce(jnp.maximum, tops)
         return top, functools.reduce(jnp.add, [s * jnp.exp(t - top) for s, t in zip(sums, tops)])
 
-    def spread(buf, sems, me, top, total, moves, slot):
+    def spread(buf, sems, me, top, total, moves, slot, between):
         buf[me] = jnp.zeros((16, UT), F32)
         buf[me, 0:NU, :] = top
         buf[me, NU:2 * NU, :] = total
         for i, move in enumerate(moves):
             go(remote(buf.at[me], buf.at[me], sems, (i,), to(**move)))
+        between()
         for i, move in enumerate(moves):
             at = buf.at[slot(move)]
             remote(at, at, sems, (i,), to(**move)).wait_recv()
         n = len(moves) + 1
         return merge([buf[k, 0:NU, :] for k in range(n)], [buf[k, NU:2 * NU, :] for k in range(n)])
 
+    e_forward(0, 0)
     top, total = merge(tops, sums)
-    top, total = spread(scr, scs, c, top, total, [dict(dc=1)], lambda m: 1 - c)
-    e_forward(1, 0)
-    top, total = spread(sz, szs, z, top, total, [dict(dz=d) for d in range(1, NZ)], lambda m: pz(-m["dz"]))
-    e_forward(0, 1)
-    e_send(0, 2)
-    e_send(1, 2)
-    top, total = spread(sy, sys_, y, top, total, [dict(dy=d) for d in range(1, NY)], lambda m: py(-m["dy"]))
+    top, total = spread(scr, scs, c, top, total, [dict(dc=1)], lambda m: 1 - c, lambda: None)
+
+    def between_z():
+        e_forward(1, 0)
+        e_send(0, 1)
+
+    def between_y():
+        e_send(1, 1)
+
+    moves = [dict(dz=d) for d in (4, 3, 5, 2, 6, 1, 7)]
+    top, total = spread(sz, szs, z, top, total, moves, lambda m: pz(-m["dz"]), between_z)
+    moves = [dict(dy=d) for d in (2, 1, 3)]
+    top, total = spread(sy, sys_, y, top, total, moves, lambda m: py(-m["dy"]), between_y)
     scale = vec[0:NU, :] / total
     for i in range(2 * NX):
         fac[i, 0:NU, :] = scale * jnp.exp(tops[i] - top)
 
-    def part(g, d):
+    def part(g, far):
         unit, units, _, _ = GROUPS[g]
-        size = units * UT
-        q = px(d)
-        if d == 2:
-            f_copy(q, 0, g).wait_recv()
-            f_copy(q, 1, g).wait_recv()
-        elif d != 0:
-            e_wait(1 if d == -1 else 0, g, 0 if d == -1 else 1)
-        base = q * QR
-        for b in range(2):
-            rows = pl.ds(pl.multiple_of(base + b * BR, 16), BR)
-            for u in range(units):
-                toks = pl.ds((unit + u) * UT, UT)
-                e = ex[q, b, unit + u].astype(F32)
-                score = fac[2 * q + b, pl.ds(unit + u, 1), :] * e - tgt[rows, toks].astype(F32)
-                st[rows, u * UT:(u + 1) * UT] = score.astype(BF16)
+        size, lane = units * UT, (256, 0, 256, 384)[g]
+        for k in (3,) if far else (0, 1, 2):
+            q = px(slots[k])
+            if k == 3:
+                f_copy(q, 0, g).wait_recv()
+                f_copy(q, 1, g).wait_recv()
+            elif k != 0:
+                e_wait(2 - k, g, k - 1)
+            for b in range(2):
+                rows = pl.ds(pl.multiple_of(q * QR + b * BR, 16), BR)
+                for u in range(units):
+                    toks = pl.ds((unit + u) * UT, UT)
+                    e = ex[q, b, unit + u].astype(F32)
+                    score = fac[2 * q + b, pl.ds(unit + u, 1), :] * e - tgt[rows, toks].astype(F32)
+                    here = k * QR + b * BR
+                    st[here:here + BR, lane + u * UT:lane + (u + 1) * UT] = score.astype(BF16)
 
         @pl.loop(0, 2)
         def _(i):
             at = pl.ds(pl.multiple_of(i * HD, HD), HD)
-            term = dot(wt[q, at, :], st[pl.ds(pl.multiple_of(base, 16), QR), 0:size])
-            if d == 0:
-                gp[g][at, :] = term
+            if far:
+                gp[g][at, :] += dot(wtb[at, :], st[3 * QR:VP, lane:lane + size])
             else:
-                gp[g][at, :] += term
-
-    def gw_part(g, d):
-        unit, units, _, _ = GROUPS[g]
-        size = units * UT
-        rows = pl.ds(pl.multiple_of(px(d) * QR, 16), QR)
-        term = dot(st[rows, 0:size], hc[x, pl.ds(unit * UT, size), :])
+                gp[g][at, :] = dot(wta[at, :], st[0:3 * QR, lane:lane + size])
+
+    def gw_part(g, k):
+        rows = slice(k * QR, (k + 1) * QR)
         if g == 0:
-            gw[rows, :] = term
-        elif g < NG - 1:
-            gw[rows, :] += term
+            gw[rows, :] = dot(st[rows, 256:512], hc[x, 0:256, :])
         else:
+            term = dot(st[rows, :], hc[x, 256:TOK, :])
             wv[rows, :] = (gw[rows, :] + term).astype(BF16)
-            copy = pltpu.make_async_copy(wv.at[rows], gw_ref.at[rows], go_sem.at[d % NX])
+            there = pl.ds(pl.multiple_of(px(slots[k]) * QR, 16), QR)
+            copy = pltpu.make_async_copy(wv.at[pl.ds(k * QR, QR)], gw_ref.at[there], go_sem.at[k])
             copy.start()
             return copy
 
@@ -416,28 +426,30 @@
         return GROUPS[g][2] * 16
 
     def deep(g, zz):
-        return pl.ds(pl.multiple_of((zz * GROUPS[g][2] * 2 // 8) * 8, 8), 8)
+        return pl.ds(pl.multiple_of(zz * 8, 8), 8), pl.ds(0, HD * GROUPS[g][2] // 4)
 
     def r1(g, cc):
         return remote(gp[g].at[half(cc)], cb[g], r1s, (g,), to(dc=1))
 
     def r2(g, d):
         n = tall(g)
-        src = ysum[g].at[pl.ds(pl.multiple_of(py(d) * n, 8), n)]
+        src = ysb[g].at[pl.ds(pl.multiple_of(py(d) * n, 16), n)]
         return remote(src, yb.at[g, d - 1, pl.ds(0, n)], r2s, (g, d - 1), to(dy=d))
 
     def r3(g, d):
-        return remote(zsum.at[g, deep(g, pz(d))], zb.at[g, d - 1], r3s, (g, d - 1), to(dz=d))
+        return remote(zsum.at[(g, *deep(g, pz(d)))], zb.at[(g, d - 1, *deep(g, 0))], r3s, (g, d - 1), to(dz=d))
 
     def r4(g):
-        return remote(fin.at[g], finb.at[g], r4s, (g,), to(dc=1))
+        return remote(fin.at[(g, *deep(g, 0))], finb.at[(g, *deep(g, 0))], r4s, (g,), to(dc=1))
 
     def start1(g):
         go(r1(g, 1 - c))
 
     def start2(g):
         r1(g, 1 - c).wait_recv()
-        ysum[g][...] = (gp[g][half(c), :] + cb[g][...]).T
+        total = (gp[g][half(c), :] + cb[g][...]).T
+        ysum[g][...] = total
+        ysb[g][...] = total.astype(BF16)
         for d in (1, 3, 2):
             go(r2(g, d))
 
@@ -446,83 +458,81 @@
         for d in (1, 3, 2):
             r2(g, d).wait_recv()
         mine = ysum[g][pl.ds(pl.multiple_of(y * n, 8), n), :]
-        zsum[g, 0:n] = mine + yb[g, 0, 0:n] + yb[g, 1, 0:n] + yb[g, 2, 0:n]
+        term = mine + functools.reduce(jnp.add, [yb[g, d, 0:n].astype(F32) for d in range(3)])
+        if GROUPS[g][2] == 4:
+            zsum[g] = term
+        else:
+            for k in range(2 * NZ):
+                zsum[g, 4 * k:4 * k + 4, 0:HD // 2] = term[4 * (k // 2):4 * (k // 2) + 4, HD // 2 * (k % 2):HD // 2 * (k % 2 + 1)]
         for d in (1, 7, 2, 6, 3, 5, 4):
             go(r3(g, d))
 
     def start4(g):
         for d in range(1, NZ):
             r3(g, d).wait_recv()
-        term = zsum[g, deep(g, z), :]
+        term = zsum[(g, *deep(g, z))]
         for d in range(1, NZ):
-            term += zb[g, d - 1]
-        fin[g] = term
+            term += zb[(g, d - 1, *deep(g, 0))]
+        fin[(g, *deep(g, 0))] = term
         go(r4(g))
 
     def finish(g):
         _, _, per, first = GROUPS[g]
         r4(g).wait_recv()
-        mine, other = fin[g], finb[g]
+        mine, other = fin[(g, *deep(g, 0))], finb[(g, *deep(g, 0))]
         left, right = jnp.where(c == 0, mine, other), jnp.where(c == 0, other, mine)
         for h, a in enumerate((left, right)):
             a = jnp.where(c == 0, a, jnp.concatenate([a[per:], a[:per]], axis=0))
-            if per == 2:
-                a = jnp.where(lax.rem(z, 2) == 0, a, jnp.concatenate([a[4:], a[:4]], axis=0))
-            outf[first:first + per, h * HD:(h + 1) * HD] = a[:per]
-
-    part(0, 0)
+            for k in range(4 // per):
+                w = HD * per // 4
+                outf[first:first + per, h * HD + k * w:h * HD + (k + 1) * w] = a[4 * k:4 * k + per]
+
+    e_forward(0, 1)
+    part(0, False)
+    e_send(0, 2)
+    part(0, True)
+    start1(0)
+    e_send(1, 2)
+    gw_part(0, 0)
+    gw_part(0, 1)
     e_forward(1, 1)
-    part(0, -1)
-    part(0, 1)
-    part(0, 2)
-    start1(0)
     e_send(0, 3)
+    gw_part(0, 2)
+    gw_part(0, 3)
+    start2(0)
+    part(1, False)
+    e_forward(0, 2)
     e_send(1, 3)
-    for d in (0, -1, 1, 2):
-        gw_part(0, d)
-    part(1, 0)
-    e_forward(0, 2)
-    part(1, -1)
-    part(1, 1)
-    start2(0)
     e_forward(1, 2)
-    part(1, 2)
+    part(2, False)
+    part(1, True)
     start1(1)
-    for d in (0, -1, 1, 2):
-        gw_part(1, d)
     e_forward(0, 3)
     e_forward(1, 3)
-    part(2, 0)
-    part(2, -1)
-    part(2, 1)
-    part(2, 2)
+    part(3, False)
+    start2(1)
+    part(2, True)
     start1(2)
-    start2(1)
-    for d in (0, -1, 1, 2):
-        gw_part(2, d)
-    part(3, 0)
-    part(3, -1)
-    part(3, 1)
     start3(0)
-    start2(2)
-    part(3, 2)
-    start1(3)
     for copy in loaded:
         copy.wait_send()
-    outs = [gw_part(3, 0)]
+    part(3, True)
+    start1(3)
+    outs = [gw_part(2, 0)]
+    start2(2)
+    start2(3)
+    outs.append(gw_part(2, 1))
     start3(1)
-    outs.append(gw_part(3, -1))
-    start2(3)
+    outs.append(gw_part(2, 2))
+    start3(2)
     start4(0)
-    outs.append(gw_part(3, 1))
-    start3(2)
+    start3(3)
+    outs.append(gw_part(2, 3))
     start4(1)
-    outs.append(gw_part(3, 2))
     finish(0)
-    start3(3)
     start4(2)
+    start4(3)
     finish(1)
-    start4(3)
     finish(2)
     finish(3)
     ghs[...] = outf[0:12, :].astype(BF16)
@@ -561,18 +571,20 @@
         scratch_shapes=[
             pltpu.VMEM((VP, DW), BF16),
             pltpu.VMEM((3, QR, DW), BF16),
-            pltpu.VMEM((NX, DW, QR), BF16),
+            pltpu.VMEM((DW, 3 * QR), BF16),
+            pltpu.VMEM((DW, QR), BF16),
             pltpu.VMEM((16, PW), BF16),
             pltpu.VMEM((256, 16, PW), BF16),
             pltpu.VMEM((NX, TOK, DW), BF16),
             pltpu.VMEM((NX, 2, TOK // UT, BR, UT), BF16),
             pltpu.VMEM((VP, TOK), BF16),
-            pltpu.VMEM((VP, 256), BF16),
+            pltpu.VMEM((VP, 512), BF16),
             pltpu.VMEM((VP, DW), F32),
             [pltpu.VMEM((DW, n * UT), F32) for _, n, _, _ in GROUPS],
             [pltpu.VMEM((HD, n * UT), F32) for _, n, _, _ in GROUPS],
             [pltpu.VMEM((n * UT, HD), F32) for _, n, _, _ in GROUPS],
-            pltpu.VMEM((NG, 3, 64, HD), F32),
+            [pltpu.VMEM((n * UT, HD), BF16) for _, n, _, _ in GROUPS],
+            pltpu.VMEM((NG, 3, 64, HD), BF16),
             pltpu.VMEM((NG, 64, HD), F32),
             pltpu.VMEM((NG, 7, 8, HD), F32),
             pltpu.VMEM((NG, 8, HD), F32),

time: 127 us -> 121 us (0.953)
  Pallas kernels: 126 us -> 120 us
    pallas_call x1, Pallas kernels: 124 us -> 117 us  [local(): pl.pallas_call(kernel, grid=(1,), out_shape=(pltpu.VMEM((VP, DW), BF16),...]
where the time goes in v3:
time: 121 us
  Pallas kernels  120 us (99%)
    pallas_call x1, Pallas kernels, local(): pl.pallas_call(kernel, grid=(1,), out_shape=(pltpu.VMEM((VP, DW), BF16),...  117 us

profile of v3, /device:TPU:1, one launch (start us, length us, event | category | flops | bytes accessed | tf_op | source)
XLA Modules:
  0.0 120.6 jit_solution(5620956366749818520)
XLA Ops:
  0.6 117.5 %head_backward.1 = (bf16[2432,1024]{1,0:T(8,128)(2,1)S(1)}, bf16[12,1024]{1,0:T(8,128)(2,1)S(1)}) custom-call(bf16[12,1024]{1,0:T(8,128)(2,1)} %hid_ref.1, bf16[2374,1024]{1,0:T(8,128)(2,1)} %w_ref.1, bf16[2374,1024]{1,0:T(8,128)(2,1)} %w_ref.1, s32[64,768]{1,0:T(8,128)} %bitcast.2, f32[64,768]{1,0:T(8,128)} %bitcast.3, f32[768]{0:T(1024)} %tw_ref.1), custom_call_target="tpu_custom_call" | custom-call | tf_op jit(solution)/shard_map/head_backward/pallas_call | solution.py:561
  118.1 2.3 %results.1 = (bf16[2374,1024]{1,0:T(8,128)(2,1)}, bf16[12,1024]{1,0:T(8,128)(2,1)}) custom-call(bf16[2432,1024]{1,0:T(8,128)(2,1)S(1)} %get-tuple-element.6.gw_ref, bf16[12,1024]{1,0:T(8,128)(2,1)S(1)} %get-tuple-element.7.gh_ref), custom_call_target="tpu_custom_call" | custom-call | tf_op jit(solution)/shard_map/results/pallas_call | solution.py:617

commit v4 on v3

--- a/solution.py
+++ b/solution.py
@@ -15,6 +15,7 @@
 NG = len(GROUPS)
 VL, QR, BR = 2374, 608, 304
 VP = NX * QR
+HALVES = ((0, 160), (160, 144))
 DW = 1024
 HD = DW // 2
 PW = 768
@@ -47,8 +48,8 @@
 def kernel(
     hid_ref, edge_ref, w_ref, ids_ref, probs_ref, tw_ref, gw_ref, gh_ref,
     wv, wq, wta, wtb, pack, hp, hc, ex, tgt, st, gw, gp, cb, ysum, ysb, yb, zsum, zb, fin, finb, outf, ghs,
-    sraw, sown, sx, scr, sz, sy, fac, idr, prr, twr, idp, wpp, vec,
-    wl_sem, hl_sem, go_sem, xs, ws, ays, azs, bzs, bys, acs, bcs, es, fs, sxs, scs, szs, sys_, r1s, r2s, r3s, r4s,
+    psend, precv, sraw, sown, sx, scr, sz, sy, fac, idr, prr, twr, idp, wpp, vec,
+    wl_sem, hl_sem, go_sem, xs, ws, ps, ays, azs, bzs, bys, acs, bcs, es, fs, sxs, scs, szs, sys_, r1s, r2s, r3s, r4s,
 ):
     v = lax.axis_index("vocab")
     x = lax.axis_index("hid")
@@ -114,17 +115,28 @@
     for copy in loads:
         copy.wait()
 
-    def w_copy(b, d):
-        q = px(d)
-        return remote(
-            wv.at[pl.ds(pl.multiple_of(q * QR + b * BR, 16), BR)], wq.at[d - 1, pl.ds(b * BR, BR)],
-            ws, (b, d - 1), to(dx=d),
-        )
-
-    for b in range(2):
-        for d in (1, 3, 2):
-            go(w_copy(b, d))
-    loaded = [pending.pop() for _ in range(6)]
+    def w_copy(d):
+        src = wv.at[pl.ds(pl.multiple_of(px(d) * QR, 16), BR)]
+        return remote(src, wq.at[d - 1, pl.ds(0, BR)], ws, (0, d - 1), to(dx=d))
+
+    ways = ((1, 2, 0), (-1, 2, 1), (-1, -1, 0), (1, 1, 1))
+
+    def h_at(j):
+        way, _, part = ways[j]
+        first, n = HALVES[part]
+        return wq.at[0 if way == 1 else 2, pl.ds(BR + first, n)]
+
+    def h_copy(j):
+        way, quarter, part = ways[j]
+        first, n = HALVES[part]
+        src = wv.at[pl.ds(pl.multiple_of(px(quarter) * QR + BR + first, 16), n)]
+        return remote(src, h_at(j), ws, (1, j), to(dx=way))
+
+    for d in (1, 3, 2):
+        go(w_copy(d))
+    for j in range(4):
+        go(h_copy(j))
+    loaded = [pending.pop() for _ in range(7)]
 
     for copy in smalls:
         copy.wait()
@@ -251,9 +263,8 @@
         start += 16 * per
     perm = jnp.where(col == pick, 1.0, 0.0).astype(BF16)
 
-    @pl.loop(0, NX * NY)
-    def _(i):
-        q, yy = i // NY, lax.rem(i, NY)
+    def unpack(k, yy):
+        q = px(k)
         parts = []
         for cc in range(NC):
             for zz in range(NZ):
@@ -266,29 +277,47 @@
             hc[q, here, 0:PW] = rows[begins[g]:begins[g] + n]
             hc[q, here, PW:DW] = rows[begins[NG + g]:begins[NG + g] + n, h:h + 256]
 
-    def w_wait(b):
-        for d in (1, 2, 3):
-            at = wq.at[d - 1, pl.ds(b * BR, BR)]
-            remote(at, at, ws, (b, d - 1), to(dx=d)).wait_recv()
-
-    def logits(b):
-        first = x * QR + b * BR
-
-        @pl.loop(0, TOK // 256)
-        def _(i):
-            toks = pl.ds(pl.multiple_of(i * 256, 256), 256)
-            total = dot(wv[pl.ds(pl.multiple_of(first, 16), BR), :], hc[x, toks, :], NT)
-            for d in (1, 2, 3):
-                total += dot(wq[d - 1, pl.ds(b * BR, BR), :], hc[px(-d), toks, :], NT)
-            real = lax.broadcasted_iota(jnp.int32, (BR, 256), 0) + first < VL
-            total = jnp.where(real, total, -1e30)
-            top = jnp.max(total, axis=0, keepdims=True)
-            shifted = jnp.exp(total - top)
-            sraw[pl.ds(b, 1), toks] = top
-            sraw[pl.ds(2 + b, 1), toks] = jnp.sum(shifted, axis=0, keepdims=True)
-            shifted = shifted.astype(BF16)
-            ex[x, b, 2 * i] = shifted[:, 0:128]
-            ex[x, b, 2 * i + 1] = shifted[:, 128:256]
+    @pl.loop(0, 3 * NY)
+    def _(i):
+        unpack(i // NY - 1, lax.rem(i, NY))
+
+    def two(quarter, part, slot, i):
+        first, n = HALVES[part]
+        toks = slice(256 * i, 256 * i + 256)
+        rows = pl.ds(pl.multiple_of(px(quarter) * QR + BR + first, 16), n)
+        other = hc[px(-1 if slot == 0 else 1), toks, :]
+        return dot(wv[rows, :], hc[x, toks, :], NT) + dot(wq[slot, BR + first:BR + first + n, :], other, NT)
+
+    def p_copy(part, i):
+        first, n = HALVES[part]
+        here = pl.ds(first, n)
+        return remote(psend.at[i, here], precv.at[i, here], ps, (part, i), to(dx=(1, -1)[part]))
+
+    def h_wait(j):
+        remote(h_at(j), h_at(j), ws, (1, j), to(dx=ways[j][0])).wait_recv()
+
+    for part_ in range(2):
+        h_wait(part_)
+        for i in range(TOK // 256):
+            first, n = HALVES[part_]
+            psend[i, first:first + n, :] = two((1, -1)[part_], part_, (0, 2)[part_], i)
+            go(p_copy(part_, i))
+
+    @pl.loop(0, NY)
+    def _(i):
+        unpack(2, i)
+
+    def numerators(b, i, total):
+        toks = pl.ds(pl.multiple_of(i * 256, 256), 256)
+        real = lax.broadcasted_iota(jnp.int32, (BR, 256), 0) + (x * QR + b * BR) < VL
+        total = jnp.where(real, total, -1e30)
+        top = jnp.max(total, axis=0, keepdims=True)
+        shifted = jnp.exp(total - top)
+        sraw[pl.ds(b, 1), toks] = top
+        sraw[pl.ds(2 + b, 1), toks] = jnp.sum(shifted, axis=0, keepdims=True)
+        shifted = shifted.astype(BF16)
+        ex[x, b, 2 * i] = shifted[:, 0:128]
+        ex[x, b, 2 * i + 1] = shifted[:, 128:256]
 
     def e_at(q, b, g):
         return ex.at[q, b, pl.ds(GROUPS[g][0], GROUPS[g][1])]
@@ -312,8 +341,24 @@
         e_wait(b, g, b)
         go(f_copy(px(-1 if b == 0 else 1), b, g))
 
-    w_wait(0)
-    logits(0)
+    for d in (1, 2, 3):
+        at = wq.at[d - 1, pl.ds(0, BR)]
+        remote(at, at, ws, (0, d - 1), to(dx=d)).wait_recv()
+
+    @pl.loop(0, TOK // 256)
+    def _(i):
+        toks = pl.ds(pl.multiple_of(i * 256, 256), 256)
+        total = dot(wv[pl.ds(pl.multiple_of(x * QR, 16), BR), :], hc[x, toks, :], NT)
+        for d in (1, 2, 3):
+            total += dot(wq[d - 1, 0:BR, :], hc[px(-d), toks, :], NT)
+        numerators(0, i, total)
+
+    h_wait(2)
+    h_wait(3)
+    for i in range(TOK // 256):
+        for part_ in range(2):
+            first, n = HALVES[part_]
+            gw[i * BR + first:i * BR + first + n, 0:256] = two(0, part_, (2, 0)[part_], i)
     for i in range(0, 3 * QR, 128):
         pieces_, j = [], i
         while j < min(i + 128, 3 * QR):
@@ -326,9 +371,15 @@
         n = min(128, QR - i)
         wtb[:, i:i + n] = wv[pl.ds(pl.multiple_of(px(2) * QR + i, 16), n), :].T
 
-    w_wait(1)
+    for i in range(TOK // 256):
+        for part_ in range(2):
+            p_copy(part_, i).wait_recv()
     e_send(0, 0)
-    logits(1)
+
+    @pl.loop(0, TOK // 256)
+    def _(i):
+        numerators(1, i, gw[pl.ds(pl.multiple_of(i * BR, 8), BR), 0:256] + precv[i])
+
 
     def sx_copy(q, d):
         return remote(sown, sx.at[q], sxs, (d - 1,), to(dx=d))
@@ -500,17 +551,17 @@
     gw_part(0, 2)
     gw_part(0, 3)
     start2(0)
+    e_send(1, 3)
     part(1, False)
     e_forward(0, 2)
-    e_send(1, 3)
     e_forward(1, 2)
     part(2, False)
     part(1, True)
     start1(1)
     e_forward(0, 3)
     e_forward(1, 3)
+    start2(1)
     part(3, False)
-    start2(1)
     part(2, True)
     start1(2)
     start3(0)
@@ -518,17 +569,17 @@
         copy.wait_send()
     part(3, True)
     start1(3)
+    start2(2)
+    start3(1)
     outs = [gw_part(2, 0)]
-    start2(2)
     start2(3)
+    start4(0)
     outs.append(gw_part(2, 1))
-    start3(1)
+    start3(2)
     outs.append(gw_part(2, 2))
-    start3(2)
-    start4(0)
     start3(3)
+    start4(1)
     outs.append(gw_part(2, 3))
-    start4(1)
     finish(0)
     start4(2)
     start4(3)
@@ -591,6 +642,8 @@
             pltpu.VMEM((NG, 8, HD), F32),
             pltpu.VMEM((16, DW), F32),
             pltpu.VMEM((12, DW), BF16),
+            pltpu.VMEM((TOK // 256, BR, 256), F32),
+            pltpu.VMEM((TOK // 256, BR, 256), F32),
             pltpu.VMEM((8, TOK), F32),
             pltpu.VMEM((4 * NU, UT), F32),
             pltpu.VMEM((NX, 4 * NU, UT), F32),
@@ -605,12 +658,12 @@
             pltpu.VMEM((TOPK, TOK), F32),
             pltpu.VMEM((8, UT), F32),
             dma((4,)), dma((3,)), dma((5,)),
-            dma((2, 3)), dma((2, 2, 3)), dma((2, 3)), dma((2, 2, 4)), dma((2, 2, 4)), dma((2, 3)), dma((2, 8)),
+            dma((2, 3)), dma((2, 2, 4)), dma((2, 2, 3)), dma((2, 3)), dma((2, 2, 4)), dma((2, 2, 4)), dma((2, 3)), dma((2, 8)),
             dma((2, 4)), dma((2, 2, 2, NG)), dma((2, 2, NG)), dma((2, 3)), dma((2, 1)), dma((2, 7)), dma((2, 3)),
             dma((2, NG)), dma((2, NG, 3)), dma((2, NG, 7)), dma((2, NG)),
         ],
         compiler_params=pltpu.CompilerParams(
-            collective_id=0, has_side_effects=True, vmem_limit_bytes=58 * 2**20
+            collective_id=0, has_side_effects=True, vmem_limit_bytes=117 * 2**19
         ),
         name="head_backward",
     )(hidden, head_weight, head_weight, teacher_ids.T, teacher_probs.T, token_weight)

time: 121 us -> 119 us (0.983)
  Pallas kernels: 120 us -> 118 us
    pallas_call x1, Pallas kernels: 117 us -> 116 us  [local(): pl.pallas_call(kernel, grid=(1,), out_shape=(pltpu.VMEM((VP, DW), BF16),...]
where the time goes in v4:
time: 119 us
  Pallas kernels  118 us (99%)
    pallas_call x1, Pallas kernels, local(): pl.pallas_call(kernel, grid=(1,), out_shape=(pltpu.VMEM((VP, DW), BF16),...  116 us

profile of v4, /device:TPU:1, one launch (start us, length us, event | category | flops | bytes accessed | tf_op | source)
XLA Modules:
  0.0 118.8 jit_solution(2419883366098291066)
XLA Ops:
  0.6 115.7 %head_backward.1 = (bf16[2432,1024]{1,0:T(8,128)(2,1)S(1)}, bf16[12,1024]{1,0:T(8,128)(2,1)S(1)}) custom-call(bf16[12,1024]{1,0:T(8,128)(2,1)} %hid_ref.1, bf16[2374,1024]{1,0:T(8,128)(2,1)} %w_ref.1, bf16[2374,1024]{1,0:T(8,128)(2,1)} %w_ref.1, s32[64,768]{1,0:T(8,128)} %bitcast.2, f32[64,768]{1,0:T(8,128)} %bitcast.3, f32[768]{0:T(1024)} %tw_ref.1), custom_call_target="tpu_custom_call" | custom-call | tf_op jit(solution)/shard_map/head_backward/pallas_call | solution.py:612
  116.3 2.3 %results.1 = (bf16[2374,1024]{1,0:T(8,128)(2,1)}, bf16[12,1024]{1,0:T(8,128)(2,1)}) custom-call(bf16[2432,1024]{1,0:T(8,128)(2,1)S(1)} %get-tuple-element.6.gw_ref, bf16[12,1024]{1,0:T(8,128)(2,1)S(1)} %get-tuple-element.7.gh_ref), custom_call_target="tpu_custom_call" | custom-call | tf_op jit(solution)/shard_map/results/pallas_call | solution.py:670

commit v5 on v4

--- a/solution.py
+++ b/solution.py
@@ -47,9 +47,9 @@
 
 def kernel(
     hid_ref, edge_ref, w_ref, ids_ref, probs_ref, tw_ref, gw_ref, gh_ref,
-    wv, wq, wta, wtb, pack, hp, hc, ex, tgt, st, gw, gp, cb, ysum, ysb, yb, zsum, zb, fin, finb, outf, ghs,
+    wv, wq, wta, wtb, pack, hp, hc, ex, tgt, st, gw, gp, gt, cb, ysb, yb, zsum, zb, outf, ghs,
     psend, precv, sraw, sown, sx, scr, sz, sy, fac, idr, prr, twr, idp, wpp, vec,
-    wl_sem, hl_sem, go_sem, xs, ws, ps, ays, azs, bzs, bys, acs, bcs, es, fs, sxs, scs, szs, sys_, r1s, r2s, r3s, r4s,
+    wl_sem, hl_sem, go_sem, xs, ws, ps, ays, azs, bzs, bys, acs, bcs, es, fs, sxs, scs, szs, sys_, r1s, r2s, r3s,
 ):
     v = lax.axis_index("vocab")
     x = lax.axis_index("hid")
@@ -146,7 +146,8 @@
     for unit, units, per, first in GROUPS:
         i = col - unit * UT
         here = (i >= 0) & (i < units * UT)
-        source = jnp.where(here, (i // per) * 12 + first + lax.rem(i, per), source)
+        chip, core = lax.rem(i // per, NY * NZ), i // (per * NY * NZ)
+        source = jnp.where(here, (chip * NC + core) * 12 + first + lax.rem(i, per), source)
     perm = jnp.where(row == source, 1.0, 0.0).astype(BF16)
     near = idr[...] - v * VL
     near = jnp.where((near >= 0) & (near < VL), near, 4095)
@@ -257,8 +258,7 @@
     for per, first in kinds:
         i = row - start
         here = (i >= 0) & (i < 16 * per)
-        zz, rest = i // (2 * per), lax.rem(i, 2 * per)
-        pick = jnp.where(here, (rest // per) * 128 + zz * 16 + first + lax.rem(rest, per), pick)
+        pick = jnp.where(here, (i // per) * 16 + first + lax.rem(i, per), pick)
         begins.append(start)
         start += 16 * per
     perm = jnp.where(col == pick, 1.0, 0.0).astype(BF16)
@@ -272,10 +272,12 @@
                 parts.append(hp[at])
         rows = dot(perm, jnp.concatenate(parts, axis=0)).astype(BF16)
         for g, (unit, _, per, first) in enumerate(GROUPS):
-            n, h = 16 * per, 256 * (first // 4)
-            here = pl.ds(pl.multiple_of(unit * UT + yy * n, 16), n)
-            hc[q, here, 0:PW] = rows[begins[g]:begins[g] + n]
-            hc[q, here, PW:DW] = rows[begins[NG + g]:begins[NG + g] + n, h:h + 256]
+            n, h = 8 * per, 256 * (first // 4)
+            for cc in range(NC):
+                here = pl.ds(pl.multiple_of(unit * UT + cc * NY * n + yy * n, 16), n)
+                a, b = begins[g] + cc * n, begins[NG + g] + cc * n
+                hc[q, here, 0:PW] = rows[a:a + n]
+                hc[q, here, PW:DW] = rows[b:b + n, h:h + 256]
 
     @pl.loop(0, 3 * NY)
     def _(i):
@@ -453,10 +455,12 @@
         @pl.loop(0, 2)
         def _(i):
             at = pl.ds(pl.multiple_of(i * HD, HD), HD)
+            held = gp[(0, 0, 1, 0)[g]]
             if far:
-                gp[g][at, :] += dot(wtb[at, :], st[3 * QR:VP, lane:lane + size])
+                total = held[at, 0:size] + dot(wtb[at, :], st[3 * QR:VP, lane:lane + size])
+                gt[g][:, at] = total.T
             else:
-                gp[g][at, :] = dot(wta[at, :], st[0:3 * QR, lane:lane + size])
+                held[at, 0:size] = dot(wta[at, :], st[0:3 * QR, lane:lane + size])
 
     def gw_part(g, k):
         rows = slice(k * QR, (k + 1) * QR)
@@ -470,17 +474,18 @@
             copy.start()
             return copy
 
-    def half(cc):
-        return pl.ds(pl.multiple_of(cc * HD, HD), HD)
+    def cores(g, cc):
+        n = GROUPS[g][1] * UT // 2
+        return pl.ds(pl.multiple_of(cc * n, 64), n)
 
     def tall(g):
-        return GROUPS[g][2] * 16
+        return GROUPS[g][2] * 8
 
     def deep(g, zz):
-        return pl.ds(pl.multiple_of(zz * 8, 8), 8), pl.ds(0, HD * GROUPS[g][2] // 4)
-
-    def r1(g, cc):
-        return remote(gp[g].at[half(cc)], cb[g], r1s, (g,), to(dc=1))
+        return pl.ds(pl.multiple_of(zz * 8, 8), 8), pl.ds(0, DW * GROUPS[g][2] // 8)
+
+    def r1(g):
+        return remote(gt[g].at[cores(g, 1 - c)], cb[g], r1s, (g,), to(dc=1))
 
     def r2(g, d):
         n = tall(g)
@@ -490,53 +495,40 @@
     def r3(g, d):
         return remote(zsum.at[(g, *deep(g, pz(d)))], zb.at[(g, d - 1, *deep(g, 0))], r3s, (g, d - 1), to(dz=d))
 
-    def r4(g):
-        return remote(fin.at[(g, *deep(g, 0))], finb.at[(g, *deep(g, 0))], r4s, (g,), to(dc=1))
-
     def start1(g):
-        go(r1(g, 1 - c))
+        go(r1(g))
 
     def start2(g):
-        r1(g, 1 - c).wait_recv()
-        total = (gp[g][half(c), :] + cb[g][...]).T
-        ysum[g][...] = total
+        r1(g).wait_recv()
+        total = gt[g][cores(g, c), :] + cb[g][...]
+        cb[g][...] = total
         ysb[g][...] = total.astype(BF16)
         for d in (1, 3, 2):
             go(r2(g, d))
 
     def start3(g):
-        n = tall(g)
+        n, per = tall(g), GROUPS[g][2]
         for d in (1, 3, 2):
             r2(g, d).wait_recv()
-        mine = ysum[g][pl.ds(pl.multiple_of(y * n, 8), n), :]
+        mine = cb[g][pl.ds(pl.multiple_of(y * n, 8), n), :]
         term = mine + functools.reduce(jnp.add, [yb[g, d, 0:n].astype(F32) for d in range(3)])
-        if GROUPS[g][2] == 4:
-            zsum[g] = term
-        else:
-            for k in range(2 * NZ):
-                zsum[g, 4 * k:4 * k + 4, 0:HD // 2] = term[4 * (k // 2):4 * (k // 2) + 4, HD // 2 * (k % 2):HD // 2 * (k % 2 + 1)]
-        for d in (1, 7, 2, 6, 3, 5, 4):
+        w = DW * per // 8
+        for zz in range(NZ):
+            for k in range(8 // per):
+                zsum[g, 8 * zz + per * k:8 * zz + per * (k + 1), 0:w] = term[per * zz:per * (zz + 1), w * k:w * (k + 1)]
+        for d in (4, 3, 5, 2, 6, 1, 7):
             go(r3(g, d))
 
-    def start4(g):
+    def finish(g):
+        _, _, per, first = GROUPS[g]
         for d in range(1, NZ):
             r3(g, d).wait_recv()
         term = zsum[(g, *deep(g, z))]
         for d in range(1, NZ):
             term += zb[(g, d - 1, *deep(g, 0))]
-        fin[(g, *deep(g, 0))] = term
-        go(r4(g))
-
-    def finish(g):
-        _, _, per, first = GROUPS[g]
-        r4(g).wait_recv()
-        mine, other = fin[(g, *deep(g, 0))], finb[(g, *deep(g, 0))]
-        left, right = jnp.where(c == 0, mine, other), jnp.where(c == 0, other, mine)
-        for h, a in enumerate((left, right)):
-            a = jnp.where(c == 0, a, jnp.concatenate([a[per:], a[:per]], axis=0))
-            for k in range(4 // per):
-                w = HD * per // 4
-                outf[first:first + per, h * HD + k * w:h * HD + (k + 1) * w] = a[4 * k:4 * k + per]
+        w = DW * per // 8
+        for k in range(8 // per):
+            outf[first:first + per, w * k:w * (k + 1)] = term[per * k:per * (k + 1)]
 
     e_forward(0, 1)
     part(0, False)
@@ -573,16 +565,12 @@
     start3(1)
     outs = [gw_part(2, 0)]
     start2(3)
-    start4(0)
     outs.append(gw_part(2, 1))
     start3(2)
     outs.append(gw_part(2, 2))
     start3(3)
-    start4(1)
     outs.append(gw_part(2, 3))
     finish(0)
-    start4(2)
-    start4(3)
     finish(1)
     finish(2)
     finish(3)
@@ -631,15 +619,13 @@
             pltpu.VMEM((VP, TOK), BF16),
             pltpu.VMEM((VP, 512), BF16),
             pltpu.VMEM((VP, DW), F32),
-            [pltpu.VMEM((DW, n * UT), F32) for _, n, _, _ in GROUPS],
-            [pltpu.VMEM((HD, n * UT), F32) for _, n, _, _ in GROUPS],
-            [pltpu.VMEM((n * UT, HD), F32) for _, n, _, _ in GROUPS],
-            [pltpu.VMEM((n * UT, HD), BF16) for _, n, _, _ in GROUPS],
-            pltpu.VMEM((NG, 3, 64, HD), BF16),
+            [pltpu.VMEM((DW, n), F32) for n in (256, 128)],
+            [pltpu.VMEM((n * UT, DW), F32) for _, n, _, _ in GROUPS],
+            [pltpu.VMEM((n * UT // 2, DW), F32) for _, n, _, _ in GROUPS],
+            [pltpu.VMEM((n * UT // 2, DW), BF16) for _, n, _, _ in GROUPS],
+            pltpu.VMEM((NG, 3, 32, DW), BF16),
             pltpu.VMEM((NG, 64, HD), F32),
             pltpu.VMEM((NG, 7, 8, HD), F32),
-            pltpu.VMEM((NG, 8, HD), F32),
-            pltpu.VMEM((NG, 8, HD), F32),
             pltpu.VMEM((16, DW), F32),
             pltpu.VMEM((12, DW), BF16),
             pltpu.VMEM((TOK // 256, BR, 256), F32),
@@ -660,7 +646,7 @@
             dma((4,)), dma((3,)), dma((5,)),
             dma((2, 3)), dma((2, 2, 4)), dma((2, 2, 3)), dma((2, 3)), dma((2, 2, 4)), dma((2, 2, 4)), dma((2, 3)), dma((2, 8)),
             dma((2, 4)), dma((2, 2, 2, NG)), dma((2, 2, NG)), dma((2, 3)), dma((2, 1)), dma((2, 7)), dma((2, 3)),
-            dma((2, NG)), dma((2, NG, 3)), dma((2, NG, 7)), dma((2, NG)),
+            dma((2, NG)), dma((2, NG, 3)), dma((2, NG, 7)),
         ],
         compiler_params=pltpu.CompilerParams(
             collective_id=0, has_side_effects=True, vmem_limit_bytes=117 * 2**19

time: 119 us -> 116 us (0.975)
  Pallas kernels: 118 us -> 115 us
    pallas_call x1, Pallas kernels: 116 us -> 113 us  [local(): pl.pallas_call(kernel, grid=(1,), out_shape=(pltpu.VMEM((VP, DW), BF16),...]
where the time goes in v5:
time: 116 us
  Pallas kernels  115 us (99%)
    pallas_call x1, Pallas kernels, local(): pl.pallas_call(kernel, grid=(1,), out_shape=(pltpu.VMEM((VP, DW), BF16),...  113 us

profile of v5, /device:TPU:1, one launch (start us, length us, event | category | flops | bytes accessed | tf_op | source)
XLA Modules:
  0.0 115.7 jit_solution(15703929350324044151)
XLA Ops:
  0.6 112.7 %head_backward.1 = (bf16[2432,1024]{1,0:T(8,128)(2,1)S(1)}, bf16[12,1024]{1,0:T(8,128)(2,1)S(1)}) custom-call(bf16[12,1024]{1,0:T(8,128)(2,1)} %hid_ref.1, bf16[2374,1024]{1,0:T(8,128)(2,1)} %w_ref.1, bf16[2374,1024]{1,0:T(8,128)(2,1)} %w_ref.1, s32[64,768]{1,0:T(8,128)} %bitcast.2, f32[64,768]{1,0:T(8,128)} %bitcast.3, f32[768]{0:T(1024)} %tw_ref.1), custom_call_target="tpu_custom_call" | custom-call | tf_op jit(solution)/shard_map/head_backward/pallas_call | solution.py:600
  113.3 2.3 %results.1 = (bf16[2374,1024]{1,0:T(8,128)(2,1)}, bf16[12,1024]{1,0:T(8,128)(2,1)}) custom-call(bf16[2432,1024]{1,0:T(8,128)(2,1)S(1)} %get-tuple-element.6.gw_ref, bf16[12,1024]{1,0:T(8,128)(2,1)S(1)} %get-tuple-element.7.gh_ref), custom_call_target="tpu_custom_call" | custom-call | tf_op jit(solution)/shard_map/results/pallas_call | solution.py:656
